TPU v7x, 512 devices: a whole 4x8x8 slice. The times are simulated.
512 devices in a mesh: cluster: 32 (over z, x), member: 16 (over y, core).
Axes of the slice: x: 4, y: 8, z: 8, core: 2. Of those that a mesh axis runs over, the one named last changes fastest.
Arguments:
- dual_ops: bfloat16 [32, 16, 1024, 1024], P('cluster', 'member')
- dual_rhs: float32 [32, 16, 1024, 128], P('cluster', 'member'), may hold values from -6 to 6
- rigid_modes: float32 [32, 16, 6, 1024], P('cluster', 'member'), may hold values from -6 to 6
- coarse_rows: float32 [32, 16, 6, 3072], P('cluster', 'member')
- start_coeffs: float32 [32, 16, 6, 128], P('cluster', 'member'), may hold values from -4 to 4
- face_counts: int32 [32, 16, 4], P('cluster', 'member'), may hold values from 0 to 64, as said below
Outputs:
- multipliers: float32 [32, 16, 1024, 128], P('cluster', 'member')
- projected: float32 [32, 16, 1024, 128], P('cluster', 'member')
Inputs may be any that keep to these rules, and one draw needn't show every extreme that they name: `face_counts`: equal on both sides of a face, zero on faces at the slab's edges; some face holds exactly 64.
All inputs are finite; a program needn't handle non-finite values.
Results may differ from a plain program's by a relative error of at most 0.0027.
Values sent between devices are 32-bit elements; how exact they have to be, the bound alone decides.
A program may use at most 64 MiB of HBM per device.

v0:
```python
import jax
import jax.numpy as jnp
from jax import lax
from jax.sharding import PartitionSpec as P

CAP = 64
ITERS = 2


HIGH = lax.Precision.HIGHEST


def extended(value, sides, width):
    for axis, dim in sides:
        size, length = (lax.axis_size(axis), value.shape[dim])
        up = [(i, (i + 1) % size) for i in range(size - 1)]
        down = [(j, i) for i, j in up]
        last = lax.slice_in_dim(value, length - width, length, axis=dim)
        leading = lax.slice_in_dim(value, 0, width, axis=dim)
        before = lax.ppermute(last, axis, up)
        after = lax.ppermute(leading, axis, down)
        value = jnp.concatenate([before, value, after], axis=dim)
    return value


def starts_of(counts):
    first = counts[0] * 0
    return [first, counts[0], counts[0] + counts[1], counts[0] + counts[1] + counts[2]]


def face_blocks(field, counts):
    starts = starts_of(counts)
    row_ids = jnp.arange(CAP, dtype=jnp.int32)
    blocks = []
    for face in range(4):
        part_rows = lax.dynamic_slice_in_dim(field, starts[face], CAP, 0)
        blocks.append(
            jnp.where((row_ids < counts[face])[:, None], part_rows, jnp.zeros_like(part_rows))
        )
    return jnp.stack(blocks)


def subtract_faces(field, counts, received):
    starts = starts_of(counts)
    row_ids = jnp.arange(CAP, dtype=jnp.int32)
    for face in range(4):
        start = starts[face]
        part_rows = lax.dynamic_slice_in_dim(field, start, CAP, 0)
        taken = jnp.where(
            (row_ids < counts[face])[:, None], received[face], jnp.zeros_like(part_rows)
        )
        field = lax.dynamic_update_slice_in_dim(field, part_rows - taken, start, 0)
    return field


def assemble(field, counts):
    blocks = face_blocks(field, counts)
    padded = extended(blocks[None, None], (("cluster", 0), ("member", 1)), 1)
    received = [padded[0, 1, 1], padded[2, 1, 0], padded[1, 0, 3], padded[1, 2, 2]]
    return subtract_faces(field, counts, received)


def per_device(dual_ops, dual_rhs, rigid_modes, coarse_rows, start_coeffs, face_counts):
    operator = dual_ops[0, 0]
    rhs_local = dual_rhs[0, 0]
    modes = rigid_modes[0, 0]
    rows_here = coarse_rows[0, 0]
    counts = face_counts[0, 0]
    slot_ids = jnp.arange(operator.shape[0], dtype=jnp.int32)
    weights = jnp.where(slot_ids < jnp.sum(counts), 0.5, 1.0).astype(jnp.float32)[:, None]

    def apply_dual(field):
        return jnp.dot(operator, field.astype(jnp.bfloat16), preferred_element_type=jnp.float32)

    def expand_modes(coeffs):
        return jnp.dot(modes.T, coeffs, precision=HIGH, preferred_element_type=jnp.float32)

    def inner_product(left, right):
        return lax.psum(jnp.sum(weights * left * right, 0), ("cluster", "member"))

    def add_products(piece):
        count = piece.shape[0]
        return jnp.dot(
            rows_here,
            piece.reshape(count * 6, -1),
            precision=HIGH,
            preferred_element_type=jnp.float32,
        )

    def coarse_coeffs(field):
        local = jnp.dot(modes, field, precision=HIGH, preferred_element_type=jnp.float32)
        return add_products(
            lax.all_gather(local.reshape(1, -1), ("cluster", "member"), axis=0, tiled=True)
        )

    multipliers = assemble(expand_modes(start_coeffs[0, 0]), counts)
    residual = assemble(rhs_local - apply_dual(multipliers), counts)
    coeffs = coarse_coeffs(residual)
    projected = residual - assemble(expand_modes(coeffs), counts)
    direction = projected
    norm_now = inner_product(projected, projected)
    for iteration in range(ITERS):
        image = assemble(apply_dual(direction), counts)
        curvature = inner_product(direction, image)
        alpha = norm_now / curvature
        multipliers = multipliers + alpha * direction
        residual = residual - alpha * image
        coeffs = coarse_coeffs(residual)
        projected = residual - assemble(expand_modes(coeffs), counts)
        norm_next = inner_product(projected, projected)
        direction = projected + norm_next / norm_now * direction
        norm_now = norm_next
    return (multipliers[None, None], projected[None, None])


def solution(mesh):
    placed = (
        P("cluster", "member", None, None),
        P("cluster", "member", None, None),
        P("cluster", "member", None, None),
        P("cluster", "member", None, None),
        P("cluster", "member", None, None),
        P("cluster", "member", None),
    )
    return jax.shard_map(
        per_device,
        mesh=mesh,
        in_specs=placed,
        out_specs=(P("cluster", "member", None, None), P("cluster", "member", None, None)),
        check_vma=False,
    )
```

profile of v0, /device:TPU:1, one launch (start us, length us, event | category | flops | bytes accessed | tf_op | source)
XLA Modules:
  0.0 885.5 jit_solution(13735131211757055342)
XLA Ops:
  7.2 1.5 fusion.111
  14.5 1.7 fusion.99
  17.0 4.0 collective-permute-start
  22.9 3.8 collective-permute-done.1
  26.7 5.2 collective-permute-start.2
  31.9 4.1 collective-permute-start.3
  37.8 3.2 collective-permute-done.3
  41.4 1.9 fusion.9
  43.5 3.1 collective-permute-start.4
  48.6 3.8 collective-permute-done.5
  52.4 4.0 collective-permute-start.6
  56.4 1.9 collective-permute-start.7
  58.9 2.3 collective-permute-done.6
  62.3 3.3 collective-permute-done.7
  67.9 123.5 %all-gather.7.cloned.1.call-done = f32[512,1,768]{2,1,0:T(1,128)} async-done(((f32[1,1,768]{2,1,0:T(1,128)}), f32[512,1,768]{2,1,0:T(1,128)}) %all-gather.7.cloned.1.call-update) | async-done | bytes 1572880 | tf_op jit(solution)/shard_map/all_gather | solution.py:93
  191.5 4.0 fusion.22
  195.5 1.8 fusion.96
  199.1 3.3 collective-permute-start.8
  204.9 3.8 collective-permute-done.9
  208.8 4.1 collective-permute-start.10
  212.8 1.9 collective-permute-start.11
  214.8 1.5 fusion.71
  217.1 1.4 dynamic_update_slice.93
  219.4 1.4 dynamic_update_slice.94
  222.9 1.4 dynamic_update_slice.95
  226.4 3.1 collective-permute-start.12
  232.1 3.2 collective-permute-done.13
  235.3 1.7 pad_maximum_fusion.3
  237.0 4.5 collective-permute-start.14
  241.5 1.9 collective-permute-start.15
  244.7 1.8 collective-permute-done.14
  247.7 3.2 collective-permute-done.15
  252.3 102.1 %all-reduce = (f32[128]{0:T(128)S(1)}, f32[128]{0:T(128)S(1)}) all-reduce(f32[128]{0:T(128)S(1)} %get-tuple-element.3, f32[128]{0:T(128)S(1)} %get-tuple-element.2), channel_id=1, replica_groups=mesh['cluster'=32,'member'=16] {'cluster','member'}, use_global_device_ids=true, to_apply=%region_2.3 | all-reduce | flops 256 | bytes 2048 | tf_op jit(solution)/shard_map/psum | solution.py:79
  357.5 111.2 %all-gather.9.cloned.1.call-done = f32[512,1,768]{2,1,0:T(1,128)} async-done(((f32[1,1,768]{2,1,0:T(1,128)}), f32[512,1,768]{2,1,0:T(1,128)}) %all-gather.9.cloned.1.call-update) | async-done | bytes 1572880 | tf_op jit(solution)/shard_map/all_gather | solution.py:93
  468.7 4.0 fusion.20
  473.9 3.3 collective-permute-start.16
  479.8 3.8 collective-permute-done.17
  484.4 4.0 collective-permute-start.18
  488.4 1.9 collective-permute-start.19
  491.3 1.4 dynamic_update_slice.101
  494.3 1.4 dynamic_update_slice.102
  495.7 2.1 collective-permute-done.19
  498.7 1.4 dynamic_update_slice.103
  500.1 2.0 fusion.14
  502.1 99.5 %psum.30 = f32[128]{0:T(128)S(1)} all-reduce(f32[128]{0:T(128)S(1)} %get-tuple-element.6), channel_id=1, replica_groups=mesh['cluster'=32,'member'=16] {'cluster','member'}, use_global_device_ids=true, to_apply=%region_6.7 | all-reduce | flops 128 | bytes 1024 | tf_op jit(solution)/shard_map/psum | solution.py:79
  601.6 1.8 fusion.4
  603.5 1.6 collective-permute-start.20
  607.3 3.6 collective-permute-done.21
  611.6 3.4 collective-permute-start.22
  615.0 2.7 collective-permute-start.23
  618.6 1.4 dynamic_update_slice.105
  620.9 1.4 dynamic_update_slice.106
  622.4 2.0 collective-permute-done.23
  625.3 1.4 dynamic_update_slice.107
  628.2 104.1 %psum.31 = f32[128]{0:T(128)S(1)} all-reduce(f32[128]{0:T(128)S(1)} %multiply_reduce_fusion), channel_id=1, replica_groups=mesh['cluster'=32,'member'=16] {'cluster','member'}, use_global_device_ids=true, to_apply=%region_8.9 | all-reduce | flops 128 | bytes 1024 | tf_op jit(solution)/shard_map/psum | solution.py:79
  732.3 1.5 convolution_bitcast_fusion
  734.4 111.5 %all-gather.11.cloned.1.call-done = f32[512,1,768]{2,1,0:T(1,128)} async-done(((f32[1,1,768]{2,1,0:T(1,128)}), f32[512,1,768]{2,1,0:T(1,128)}) %all-gather.11.cloned.1.call-update) | async-done | bytes 1572880 | tf_op jit(solution)/shard_map/all_gather | solution.py:93
  845.8 4.0 fusion.18
  851.1 3.3 collective-permute-start.24
  856.9 3.8 collective-permute-done.25
  860.8 4.0 collective-permute-start.26
  864.8 1.9 collective-permute-start.27
  869.7 1.5 fusion.30
  876.3 2.6 subtract_bitcast_fusion
  (135 shorter events, 60.1 us)
Async XLA Ops:
  7.2 34.2 %copy-start = (bf16[1,1,1024,1024]{3,2,1,0:T(8,128)(2,1)S(1)}, bf16[1,1,1024,1024]{3,2,1,0:T(8,128)(2,1)}, u32[]{:S(2)}) copy-start(bf16[1,1,1024,1024]{3,2,1,0:T(8,128)(2,1)} %param.6) | copy-start | bytes 6291460
  7.2 184.3 %all-gather.7.cloned.1.call-start = ((), (), s32[]{:S(2)}) async-start(), calls=%async_computation | async-start | bytes 1575936 | tf_op jit(solution)/shard_map/all_gather | solution.py:93
  17.0 5.9 collective-permute-start
  20.9 5.7 collective-permute-start.1
  26.7 9.9 %collective-permute-start.2 = (f32[3,1,4,64,128]{4,3,2,1,0:T(8,128)S(1)}, f32[3,1,4,64,128]{4,3,2,1,0:T(8,128)}, u32[]{:S(2)}, u32[]{:S(2)}) collective-permute-start(f32[3,1,4,64,128]{4,3,2,1,0:T(8,128)S(1)} %pad_maximum_fusion), channel_id=1, source_target_pairs={{0,1},{1,2},{2,3},{3,4},{4,5},{5,6},{6,7},{7,8},{8,9},{9,10},{10,1... | collective-permute-start | bytes 1179656 | tf_op jit(solution)/shard_map/ppermute | solution.py:20
  31.9 9.1 %collective-permute-start.3 = (f32[3,1,4,64,128]{4,3,2,1,0:T(8,128)S(1)}, f32[3,1,4,64,128]{4,3,2,1,0:T(8,128)S(1)}, u32[]{:S(2)}, u32[]{:S(2)}) collective-permute-start(f32[3,1,4,64,128]{4,3,2,1,0:T(8,128)S(1)} %pad_maximum_fusion), channel_id=1, source_target_pairs={{1,0},{2,1},{3,2},{4,3},{5,4},{6,5},{7,6},{8,7},{9,8},{10,9},{11,1... | collective-permute-start | bytes 1179656 | tf_op jit(solution)/shard_map/ppermute | solution.py:21
  41.4 2.0 copy-start.3
  43.4 23.5 %copy-start.7 = (f32[1,1,6,1024]{3,1,2,0:T(1,128)S(1)}, f32[1,1,6,1024]{3,1,2,0:T(1,128)}, u32[]{:S(2)}) copy-start(f32[1,1,6,1024]{3,1,2,0:T(1,128)} %param.8) | copy-start | bytes 73732
  43.4 148.1 %copy-start.8 = (f32[1,1,6,3072]{3,1,2,0:T(1,128)S(1)}, f32[1,1,6,3072]{3,1,2,0:T(1,128)}, u32[]{:S(2)}) copy-start(f32[1,1,6,3072]{3,1,2,0:T(1,128)} %param.9) | copy-start | bytes 221188
  43.5 5.1 collective-permute-start.4
  46.7 5.7 collective-permute-start.5
  52.4 8.7 collective-permute-start.6
  56.4 9.2 %collective-permute-start.7 = (f32[3,1,4,64,128]{4,3,2,1,0:T(8,128)S(1)}, f32[3,1,4,64,128]{4,3,2,1,0:T(8,128)}, u32[]{:S(2)}, u32[]{:S(2)}) collective-permute-start(f32[3,1,4,64,128]{4,3,2,1,0:T(8,128)S(1)} %pad_maximum_fusion.1), channel_id=1, source_target_pairs={{1,0},{2,1},{3,2},{4,3},{5,4},{6,5},{7,6},{8,7},{9,8},{10,9},{11,1... | collective-permute-start | bytes 1179656 | tf_op jit(solution)/shard_map/ppermute | solution.py:21
  66.8 157.5 %copy-start.1 = (f32[1024,128]{1,0:T(8,128)}, f32[1024,128]{1,0:T(8,128)S(1)}, u32[]{:S(2)}) copy-start(f32[1024,128]{1,0:T(8,128)S(1)} %dynamic_update_slice.91) | copy-start | bytes 1572868
  67.9 400.8 %all-gather.9.cloned.1.call-start = ((), (), s32[]{:S(2)}) async-start(), calls=%async_computation.1 | async-start | bytes 1575936 | tf_op jit(solution)/shard_map/all_gather | solution.py:93
  199.1 5.8 collective-permute-start.8
  202.4 6.4 collective-permute-start.9
  208.8 9.7 %collective-permute-start.10 = (f32[3,1,4,64,128]{4,3,2,1,0:T(8,128)S(1)}, f32[3,1,4,64,128]{4,3,2,1,0:T(8,128)}, u32[]{:S(2)}, u32[]{:S(2)}) collective-permute-start(f32[3,1,4,64,128]{4,3,2,1,0:T(8,128)S(1)} %pad_maximum_fusion.2), channel_id=1, source_target_pairs={{0,1},{1,2},{2,3},{3,4},{4,5},{5,6},{6,7},{7,8},{8,9},{9,10},{10,1... | collective-permute-start | bytes 1179656 | tf_op jit(solution)/shard_map/ppermute | solution.py:20
  212.8 9.2 %collective-permute-start.11 = (f32[3,1,4,64,128]{4,3,2,1,0:T(8,128)S(1)}, f32[3,1,4,64,128]{4,3,2,1,0:T(8,128)}, u32[]{:S(2)}, u32[]{:S(2)}) collective-permute-start(f32[3,1,4,64,128]{4,3,2,1,0:T(8,128)S(1)} %pad_maximum_fusion.2), channel_id=1, source_target_pairs={{1,0},{2,1},{3,2},{4,3},{5,4},{6,5},{7,6},{8,7},{9,8},{10,9},{11,1... | collective-permute-start | bytes 1179656 | tf_op jit(solution)/shard_map/ppermute | solution.py:21
  225.5 5.3 copy-start.9
  226.4 5.7 collective-permute-start.12
  229.5 5.8 collective-permute-start.13
  237.0 9.5 %collective-permute-start.14 = (f32[3,1,4,64,128]{4,3,2,1,0:T(8,128)}, f32[3,1,4,64,128]{4,3,2,1,0:T(8,128)}, u32[]{:S(2)}, u32[]{:S(2)}) collective-permute-start(f32[3,1,4,64,128]{4,3,2,1,0:T(8,128)} %pad_maximum_fusion.3), channel_id=1, source_target_pairs={{0,1},{1,2},{2,3},{3,4},{4,5},{5,6},{6,7},{7,8},{8,9},{9,10},{10,1... | collective-permute-start | bytes 1179656 | tf_op jit(solution)/shard_map/ppermute | solution.py:20
  241.5 9.4 %collective-permute-start.15 = (f32[3,1,4,64,128]{4,3,2,1,0:T(8,128)}, f32[3,1,4,64,128]{4,3,2,1,0:T(8,128)}, u32[]{:S(2)}, u32[]{:S(2)}) collective-permute-start(f32[3,1,4,64,128]{4,3,2,1,0:T(8,128)} %pad_maximum_fusion.3), channel_id=1, source_target_pairs={{1,0},{2,1},{3,2},{4,3},{5,4},{6,5},{7,6},{8,7},{9,8},{10,9},{11,1... | collective-permute-start | bytes 1179656 | tf_op jit(solution)/shard_map/ppermute | solution.py:21
  252.1 102.3 %copy-start.4 = (f32[1024,128]{1,0:T(8,128)}, f32[1024,128]{1,0:T(8,128)S(1)}, u32[]{:S(2)}) copy-start(f32[1024,128]{1,0:T(8,128)S(1)} %dynamic_update_slice.99) | copy-start | bytes 1572868
  354.4 0.6 copy-start.11
  357.3 488.6 %all-gather.11.cloned.1.call-start = ((), (), s32[]{:S(2)}) async-start(), calls=%async_computation.2 | async-start | bytes 1575936 | tf_op jit(solution)/shard_map/all_gather | solution.py:93
  473.9 5.9 collective-permute-start.16
  477.2 6.4 collective-permute-start.17
  484.4 9.0 %collective-permute-start.18 = (f32[3,1,4,64,128]{4,3,2,1,0:T(8,128)}, f32[3,1,4,64,128]{4,3,2,1,0:T(8,128)}, u32[]{:S(2)}, u32[]{:S(2)}) collective-permute-start(f32[3,1,4,64,128]{4,3,2,1,0:T(8,128)} %pad_maximum_fusion.4), channel_id=1, source_target_pairs={{0,1},{1,2},{2,3},{3,4},{4,5},{5,6},{6,7},{7,8},{8,9},{9,10},{10,1... | collective-permute-start | bytes 1179656 | tf_op jit(solution)/shard_map/ppermute | solution.py:20
  488.4 9.4 %collective-permute-start.19 = (f32[3,1,4,64,128]{4,3,2,1,0:T(8,128)}, f32[3,1,4,64,128]{4,3,2,1,0:T(8,128)}, u32[]{:S(2)}, u32[]{:S(2)}) collective-permute-start(f32[3,1,4,64,128]{4,3,2,1,0:T(8,128)} %pad_maximum_fusion.4), channel_id=1, source_target_pairs={{1,0},{2,1},{3,2},{4,3},{5,4},{6,5},{7,6},{8,7},{9,8},{10,9},{11,1... | collective-permute-start | bytes 1179656 | tf_op jit(solution)/shard_map/ppermute | solution.py:21
  490.4 0.8 copy-start.6
  601.6 25.2 %copy-start.10 = (f32[128]{0:T(128)}, f32[128]{0:T(128)S(1)}, u32[]{:S(2)}) copy-start(f32[128]{0:T(128)S(1)} %div.10) | copy-start | bytes 1540
  603.5 3.8 collective-permute-start.20
  605.1 5.7 collective-permute-start.21
  611.6 8.5 collective-permute-start.22
  615.0 9.4 %collective-permute-start.23 = (f32[3,1,4,64,128]{4,3,2,1,0:T(8,128)}, f32[3,1,4,64,128]{4,3,2,1,0:T(8,128)}, u32[]{:S(2)}, u32[]{:S(2)}) collective-permute-start(f32[3,1,4,64,128]{4,3,2,1,0:T(8,128)} %pad_maximum_fusion.5), channel_id=1, source_target_pairs={{1,0},{2,1},{3,2},{4,3},{5,4},{6,5},{7,6},{8,7},{9,8},{10,9},{11,1... | collective-permute-start | bytes 1179656 | tf_op jit(solution)/shard_map/ppermute | solution.py:21
  617.8 0.8 copy-start.2
  732.3 118.6 %copy-start.12 = (f32[128]{0:T(128)}, f32[128]{0:T(128)S(1)}, u32[]{:S(2)}) copy-start(f32[128]{0:T(128)S(1)} %div.11) | copy-start | bytes 1540
  851.1 5.9 collective-permute-start.24
  854.3 6.4 collective-permute-start.25
  860.8 9.0 %collective-permute-start.26 = (f32[3,1,4,64,128]{4,3,2,1,0:T(8,128)S(1)}, f32[3,1,4,64,128]{4,3,2,1,0:T(8,128)}, u32[]{:S(2)}, u32[]{:S(2)}) collective-permute-start(f32[3,1,4,64,128]{4,3,2,1,0:T(8,128)S(1)} %pad_maximum_fusion.6), channel_id=1, source_target_pairs={{0,1},{1,2},{2,3},{3,4},{4,5},{5,6},{6,7},{7,8},{8,9},{9,10},{10,1... | collective-permute-start | bytes 1179656 | tf_op jit(solution)/shard_map/ppermute | solution.py:20
  864.8 9.2 %collective-permute-start.27 = (f32[3,1,4,64,128]{4,3,2,1,0:T(8,128)S(1)}, f32[3,1,4,64,128]{4,3,2,1,0:T(8,128)}, u32[]{:S(2)}, u32[]{:S(2)}) collective-permute-start(f32[3,1,4,64,128]{4,3,2,1,0:T(8,128)S(1)} %pad_maximum_fusion.6), channel_id=1, source_target_pairs={{1,0},{2,1},{3,2},{4,3},{5,4},{6,5},{7,6},{8,7},{9,8},{10,9},{11,1... | collective-permute-start | bytes 1179656 | tf_op jit(solution)/shard_map/ppermute | solution.py:21
  866.8 0.8 copy-start.5
Sparse Core Ops, SparseCore 0:
  68.0 123.4 all-gather.6
  357.4 111.2 all-gather.8
  734.5 111.2 all-gather.10
where the time goes:
time: 890 us; the launch traced here: 885 us
  waiting for transfers between devices  399 us (45%)
  blocking collectives  306 us (34%)
  starting transfers between devices  76.5 us (9%)
  other arithmetic  34.9 us (4%)
  local copies, waits for them, and re-layouts  26.7 us (3%)
  matrix products  24.2 us (3%)
  between operations  18.3 us (2%)
    all_gather x3, waiting for transfers between devices, coarse_coeffs(): lax.all_gather(local.reshape(1, -1), ('cluster', 'member'), axis=0, tiled...  346 us
    psum x3, blocking collectives, inner_product(): return lax.psum(jnp.sum(weights * left * right, 0), ('cluster', 'member'))  306 us
    ppermute x14, starting transfers between devices, extended(): before = lax.ppermute(last, axis, up)  50.8 us
    ppermute x14, waiting for transfers between devices, extended(): after = lax.ppermute(leading, axis, down)  42.2 us
    ppermute x14, starting transfers between devices, extended(): after = lax.ppermute(leading, axis, down)  25.4 us
    dynamic_update_slice x21, local copies, waits for them, and re-layouts, subtract_faces(): field = lax.dynamic_update_slice_in_dim(field, part_rows - taken, start, 0)  20.4 us
  transfers between devices with their start and end apart: 31, of which 27 were waited for; matrix products, arithmetic and copies ran while one was open for 3% of the time, Pallas kernels for 0%

commit v1 on v0

v1 whole, which is shorter than its diff:
```python
import functools

import jax
import jax.numpy as jnp
from jax import lax
from jax.experimental import pallas as pl
from jax.experimental.pallas import tpu as pltpu
from jax.sharding import PartitionSpec as P

CAP = 64
TOP = 4 * CAP
MESH = pl.DeviceIdType.MESH
F32 = jnp.float32
BF16 = jnp.bfloat16


def dot(a, b):
    return jnp.dot(a, b, preferred_element_type=F32)


def split(x):
    high = x.astype(BF16)
    return high, (x - high.astype(F32)).astype(BF16)


def far_first(t, n):
    return n // 2 + ((t % 2) * 2 - 1) * ((t + 1) // 2)


def kernel(
    ncl, nme, nx,
    ops_hbm, rhs_hbm, modes_hbm, rows_hbm, start_hbm, counts,
    m_ref, p_ref,
    ops, rhs, modes, rows, start,
    b32, bb, bt, pad, hs, hb,
    v_ref, r_ref, p0_ref, u0_ref, p1_ref, im_ref,
    s1_send, s1_buf, q_send, q_buf, f_send, f_buf,
    g_buf, t_buf, t_send, c_buf, g3_buf, t3_buf, t3_send,
    local_sem, s1_sems, h_sems, q_sems, f_sems, g_sems, t_sems, c_sems,
):
    i, j = lax.axis_index("cluster"), lax.axis_index("member")
    nz = ncl // nx
    west, east = (lax.rem(i + ncl - 1, ncl), j), (lax.rem(i + 1, ncl), j)
    south, north = (i, lax.rem(j + nme - 1, nme)), (i, lax.rem(j + 1, nme))
    sides = (west, east, south, north)

    def member_peer(t):
        return lax.rem(j + far_first(t, nme), nme)

    def cluster_peer(t):
        z = lax.rem(i // nx + far_first(t // nx, nz), nz)
        x = lax.rem(i % nx + far_first(t % nx, nx), nx)
        return z * nx + x

    def over_members(body):
        lax.fori_loop(0, nme - 1, lambda t, _: (body(member_peer(t)), 0)[1], 0)

    def over_cluster(body):
        lax.fori_loop(0, ncl - 1, lambda t, _: (body(cluster_peer(t)), 0)[1], 0)

    def send(src, dst, sems, device):
        pltpu.make_async_remote_copy(
            src, dst, sems.at[0], sems.at[1], device_id=device, device_id_type=MESH
        ).start()

    def wait(ref, sem):
        pltpu.make_async_copy(ref, ref, sem).wait()

    barrier = pltpu.get_barrier_semaphore()

    def greet(device):
        pl.semaphore_signal(barrier, inc=1, device_id=device, device_id_type=MESH)

    over_cluster(lambda peer: greet((peer, j)))
    over_members(lambda peer: greet((i, peer)))

    loads = [
        pltpu.make_async_copy(src, dst, local_sem.at[n])
        for n, (src, dst) in enumerate(
            ((modes_hbm, modes), (start_hbm, start), (rows_hbm, rows), (ops_hbm, ops), (rhs_hbm, rhs))
        )
    ]
    for load in loads:
        load.start()

    first = [counts[0] * 0, counts[0], counts[0] + counts[1], counts[0] + counts[1] + counts[2]]
    in_faces = first[3] + counts[3]
    face_rows = lax.broadcasted_iota(jnp.int32, (CAP, 128), 0)

    def face_of(ref, f):
        block = ref[pl.ds(first[f], CAP), :]
        return jnp.where(face_rows < counts[f], block, 0.0)

    pad[...] = jnp.zeros_like(pad)

    loads[0].wait()
    loads[1].wait()
    slots = modes.shape[1]
    v_ref[...] = jnp.concatenate([modes[...], jnp.zeros((122, slots), F32)], 0).T
    start8 = jnp.concatenate([start[...], jnp.zeros((2, 128), F32)], 0)
    for f in range(4):
        s1_send[f, 0:CAP, :] = face_of(v_ref, f)
        s1_send[f, CAP : CAP + 8, :] = start8

    loads[2].wait()
    wide, cols = 8 * nme, 6 * nme
    spread = (
        lax.broadcasted_iota(jnp.int32, (cols, wide), 1)
        == (lax.broadcasted_iota(jnp.int32, (cols, wide), 0) // 6) * 8
        + lax.broadcasted_iota(jnp.int32, (cols, wide), 0) % 6
    ).astype(BF16)
    stacked = jnp.concatenate(
        [
            jnp.concatenate([rows[:, k * cols : (k + 1) * cols], jnp.zeros((2, cols), F32)], 0)
            for k in range(ncl)
        ],
        0,
    )
    high, low = split(stacked)
    placed = dot(high, spread) + dot(low, spread)
    row8 = lax.broadcasted_iota(jnp.int32, (8 * ncl, wide), 0) % 8
    col8 = lax.broadcasted_iota(jnp.int32, (8 * ncl, wide), 1) % 8
    placed = placed + jnp.where((row8 == col8) & (row8 >= 6), 1.0, 0.0)
    hs[...] = placed.reshape(ncl, 8, wide)
    hb[i] = hs[i]

    pl.semaphore_wait(barrier, ncl + nme - 2)

    for f in range(4):
        send(s1_send.at[f], s1_buf.at[f ^ 1], s1_sems, sides[f])
    over_cluster(lambda peer: send(hs.at[peer], hb.at[i], h_sems, (peer, j)))

    b32[...] = v_ref[...]
    wait(s1_buf, s1_sems.at[1])
    top = b32[0:TOP, :]
    for f in range(4):
        pad[f, TOP : TOP + CAP, :] = s1_buf[f, 0:CAP, :]
    for f in range(4):
        top = top - pltpu.roll(pad[f, pl.ds(TOP - first[f], TOP), :], 8 * (f + 1), 1)
    b32[0:TOP, :] = top
    lane = lax.broadcasted_iota(jnp.int32, (slots, 128), 1)
    b_high, b_low = split(b32[...])
    b_high, b_low = b_high.astype(F32), b_low.astype(F32)
    packed = jnp.where(
        lane < 40, b_high, jnp.where(lane < 80, pltpu.roll(b_high, 40, 1), pltpu.roll(b_low, 80, 1))
    )
    bb[...] = packed.astype(BF16)
    bt[...] = packed.T.astype(BF16)

    def expand(coeffs):
        high, low = split(coeffs)
        return dot(bb[...], jnp.concatenate([high, low, high, jnp.zeros((8, 128), BF16)], 0))

    def products(field):
        high, low = split(field)
        both = dot(bt[...], high)
        return both[0:40] + both[80:120] + dot(bt[0:40, :], low)

    def assemble(ref, k):
        wait(f_buf.at[k], f_sems.at[k, 1])
        for f in range(4):
            pad[f, TOP : TOP + CAP, :] = f_buf[k, f]
        top = ref[0:TOP, :]
        for f in range(4):
            top = top - pad[f, pl.ds(TOP - first[f], TOP), :]
        ref[0:TOP, :] = top

    def send_faces(ref, k):
        for f in range(4):
            f_send[k, f] = face_of(ref, f)
            send(f_send.at[k, f], f_buf.at[k, f ^ 1], f_sems.at[k], sides[f])

    tile_row = lax.broadcasted_iota(jnp.int32, (8, 128), 0)

    def inner_rows(product):
        return jnp.sum(product, 0, keepdims=True)

    def weighted(field):
        top_rows = lax.broadcasted_iota(jnp.int32, (TOP, 128), 0)
        square = field * field
        return inner_rows(square) - 0.5 * inner_rows(
            jnp.where(top_rows < in_faces, square[0:TOP], 0.0)
        )

    def gather_modes(field, k):
        terms = products(field)
        q_send[k] = terms[8:40].reshape(4, 8, 128)
        for f in range(4):
            send(q_send.at[k, f], q_buf.at[k, f ^ 1], q_sems.at[k], sides[f])
        return terms[0:8]

    def coarse(k, own, scalars):
        wait(q_buf.at[k], q_sems.at[k, 1])
        tile = own + q_buf[k, 0] + q_buf[k, 1] + q_buf[k, 2] + q_buf[k, 3]
        for n, scalar in enumerate(scalars[:2]):
            tile = jnp.where(tile_row == 6 + n, scalar, tile)
        h_high, h_low = split(hb[...].reshape(8 * ncl, wide))
        third = len(scalars) == 3
        gathered = g3_buf if third else g_buf.at[k]
        sending = t3_send if third else t_send.at[k]
        summing = t3_buf if third else t_buf.at[k]
        if third:
            gathered[j, 0:8, :] = tile
            gathered[j, 8:9, :] = scalars[2]
        else:
            gathered[j] = tile
        over_members(lambda peer: send(gathered.at[j], gathered.at[j], g_sems.at[k], (i, peer)))
        wait(gathered.at[0 : nme - 1], g_sems.at[k, 1])
        g_high, g_low = split(gathered[:, 0:8, :].reshape(wide, 128))
        part = dot(h_high, g_high) + dot(h_high, g_low) + dot(h_low, g_high)
        sending[:, 0:8, :] = part.reshape(ncl, 8, 128)
        if third:
            last = jnp.sum(gathered[:, 8:9, :], 0, keepdims=True)
            sending[:, 8:9, :] = jnp.broadcast_to(last, (ncl, 1, 128))
        summing[i] = sending[i]
        over_cluster(lambda peer: send(sending.at[peer], summing.at[i], t_sems.at[k], (peer, j)))
        wait(summing.at[0 : ncl - 1], t_sems.at[k, 1])
        total = jnp.sum(summing[:, 0:8, :], 0)
        c_buf[k, 0] = jnp.where(tile_row < 6, total, 0.0)
        for f in range(4):
            send(c_buf.at[k, 0], c_buf.at[k, 1 + (f ^ 1)], c_sems.at[k], sides[f])
        sums = [total[6:7], total[7:8]]
        if third:
            sums.append(jnp.sum(summing[:, 8:9, :], 0))
        return sums

    def coefficients(k):
        wait(c_buf.at[k, 1:5], c_sems.at[k, 1])
        return c_buf[k].reshape(40, 128)

    starts = jnp.concatenate([start8] + [s1_buf[f, CAP : CAP + 8, :] for f in range(4)], 0)
    m_ref[...] = expand(starts)
    loads[3].wait()
    loads[4].wait()
    r_ref[...] = rhs[...] - dot(ops[...], m_ref[...].astype(BF16))
    own = gather_modes(r_ref[...], 0)
    send_faces(r_ref, 0)
    wait(hb.at[0 : ncl - 1], h_sems.at[1])
    coarse(0, own, [])
    assemble(r_ref, 0)
    coeffs0 = coefficients(0)
    p0_ref[...] = r_ref[...] - expand(coeffs0)

    u0_ref[...] = dot(ops[...], p0_ref[...].astype(BF16))
    own = gather_modes(u0_ref[...], 1)
    send_faces(u0_ref, 1)
    norm0, curv0 = coarse(
        1, own, [weighted(p0_ref[...]), inner_rows(p0_ref[...] * u0_ref[...])]
    )
    im_ref[...] = u0_ref[...]
    assemble(im_ref, 1)
    alpha0 = norm0 / curv0
    r_ref[...] = r_ref[...] - alpha0 * im_ref[...]
    image_coeffs = coefficients(1)
    coeffs1 = coeffs0 - alpha0 * image_coeffs
    p1_ref[...] = r_ref[...] - expand(coeffs1)

    high, low = split(p1_ref[...])
    v_ref[...] = dot(ops[...], high) + dot(ops[...], low)
    own = gather_modes(v_ref[...], 2)
    send_faces(v_ref, 2)
    norm1, curv1, cross = coarse(
        2,
        own,
        [
            weighted(p1_ref[...]),
            inner_rows(p1_ref[...] * v_ref[...]),
            inner_rows(p1_ref[...] * u0_ref[...] + p0_ref[...] * v_ref[...]),
        ],
    )
    beta = norm1 / norm0
    alpha1 = norm1 / (curv1 + beta * (cross + beta * curv0))
    assemble(v_ref, 2)
    m_ref[...] = m_ref[...] + (alpha0 + alpha1 * beta) * p0_ref[...] + alpha1 * p1_ref[...]
    r_ref[...] = r_ref[...] - alpha1 * (v_ref[...] + beta * im_ref[...])
    coeffs2 = coeffs1 - alpha1 * (coefficients(2) + beta * image_coeffs)
    p_ref[...] = r_ref[...] - expand(coeffs2)

    wait(s1_buf, s1_sems.at[0])
    wait(hb.at[0 : ncl - 1], h_sems.at[0])
    for k in range(3):
        wait(q_buf.at[k], q_sems.at[k, 0])
        wait(f_buf.at[k], f_sems.at[k, 0])
        gathered, summing = (g3_buf, t3_buf) if k == 2 else (g_buf.at[k], t_buf.at[k])
        wait(gathered.at[0 : nme - 1], g_sems.at[k, 0])
        wait(summing.at[0 : ncl - 1], t_sems.at[k, 0])
        wait(c_buf.at[k, 1:5], c_sems.at[k, 0])


def solution(mesh):
    ncl, nme = mesh.shape["cluster"], mesh.shape["member"]
    nx = 4 if ncl % 4 == 0 else 1

    def per_device(dual_ops, dual_rhs, rigid_modes, coarse_rows, start_coeffs, face_counts):
        slots, cases = dual_rhs.shape[2:]
        field = pltpu.VMEM((slots, cases), F32)
        out = jax.ShapeDtypeStruct((slots, cases), F32)
        multipliers, projected = pl.pallas_call(
            functools.partial(kernel, ncl, nme, nx),
            out_shape=(out, out),
            in_specs=[pl.BlockSpec(memory_space=pl.ANY)] * 5
            + [pl.BlockSpec(memory_space=pltpu.SMEM)],
            out_specs=(pl.BlockSpec(memory_space=pltpu.VMEM),) * 2,
            scratch_shapes=[
                pltpu.VMEM((slots, slots), BF16),
                field,
                pltpu.VMEM((6, slots), F32),
                pltpu.VMEM((6, 6 * ncl * nme), F32),
                pltpu.VMEM((6, cases), F32),
                field,
                pltpu.VMEM((slots, 128), BF16),
                pltpu.VMEM((128, slots), BF16),
                pltpu.VMEM((4, 2 * TOP + CAP, cases), F32),
                pltpu.VMEM((ncl, 8, 8 * nme), F32),
                pltpu.VMEM((ncl, 8, 8 * nme), F32),
                field, field, field, field, field, field,
                pltpu.VMEM((4, CAP + 8, cases), F32),
                pltpu.VMEM((4, CAP + 8, cases), F32),
                pltpu.VMEM((3, 4, 8, cases), F32),
                pltpu.VMEM((3, 4, 8, cases), F32),
                pltpu.VMEM((3, 4, CAP, cases), F32),
                pltpu.VMEM((3, 4, CAP, cases), F32),
                pltpu.VMEM((2, nme, 8, cases), F32),
                pltpu.VMEM((2, ncl, 8, cases), F32),
                pltpu.VMEM((2, ncl, 8, cases), F32),
                pltpu.VMEM((3, 5, 8, cases), F32),
                pltpu.VMEM((nme, 9, cases), F32),
                pltpu.VMEM((ncl, 9, cases), F32),
                pltpu.VMEM((ncl, 9, cases), F32),
                pltpu.SemaphoreType.DMA((5,)),
                pltpu.SemaphoreType.DMA((2,)),
                pltpu.SemaphoreType.DMA((2,)),
                pltpu.SemaphoreType.DMA((3, 2)),
                pltpu.SemaphoreType.DMA((3, 2)),
                pltpu.SemaphoreType.DMA((3, 2)),
                pltpu.SemaphoreType.DMA((3, 2)),
                pltpu.SemaphoreType.DMA((3, 2)),
            ],
            compiler_params=pltpu.CompilerParams(
                collective_id=0, has_side_effects=True, vmem_limit_bytes=48 << 20
            ),
            name="cg",
        )(
            dual_ops[0, 0], dual_rhs[0, 0], rigid_modes[0, 0], coarse_rows[0, 0],
            start_coeffs[0, 0], face_counts[0, 0],
        )
        return multipliers[None, None], projected[None, None]

    whole = P("cluster", "member", None, None)
    return jax.shard_map(
        per_device,
        mesh=mesh,
        in_specs=(whole,) * 5 + (P("cluster", "member", None),),
        out_specs=(whole, whole),
        check_vma=False,
    )
```

time: 890 us -> 95 us (0.11)
  waiting for transfers between devices: 399 us -> 0 us
  blocking collectives: 306 us -> 0 us
  Pallas kernels: 0 us -> 86.8 us
  starting transfers between devices: 76.5 us -> 0 us
  other arithmetic: 34.9 us -> 0 us
  matrix products: 24.2 us -> 0 us
  local copies, waits for them, and re-layouts: 26.7 us -> 7.2 us
  between operations: 18.3 us -> 0.65 us
    all_gather x3 -> x0, waiting for transfers between devices: 346 us -> none  [coarse_coeffs(): lax.all_gather(local.reshape(1, -1), ('cluster', 'member'), axis=0, tiled...]
    psum x3 -> x0, blocking collectives: 306 us -> none  [inner_product(): return lax.psum(jnp.sum(weights * left * right, 0), ('cluster', 'member'))]
    pallas_call x0 -> x1, Pallas kernels: none -> 86.8 us  [per_device(): pl.pallas_call(functools.partial(kernel, ncl, nme, nx), out_shape=(out, o...]
    ppermute x28 -> x0, starting transfers between devices: 76.2 us -> none  [the longest x14 50.8 us: extended(): before = lax.ppermute(last, axis, up)]
    ppermute x28 -> x0, waiting for transfers between devices: 53 us -> none  [the longest x14 42.2 us: extended(): after = lax.ppermute(leading, axis, down)]
    dot_general x13 -> x0, matrix products: 24.2 us -> none  [the longest x3 12.1 us: add_products(): jnp.dot(rows_here, piece.reshape(count * 6, -1), precision=HIGH, preferre...]
    dynamic_update_slice x21 -> x0, local copies, waits for them, and re-layouts: 20.4 us -> none  [subtract_faces(): field = lax.dynamic_update_slice_in_dim(field, part_rows - taken, start, 0)]
    sub x23 -> x0, other arithmetic: 16.8 us -> none  [the longest x21 14.5 us: subtract_faces(): field = lax.dynamic_update_slice_in_dim(field, part_rows - taken, start, 0)]
  transfers between devices with their start and end apart: 31 -> 0, of which waited for: 27 -> 0; matrix products, arithmetic and copies ran while one was open for 3% -> 0% of each run, Pallas kernels for 0% -> 0%
where the time goes in v1:
time: 95 us; the launch traced here: 94.6 us
  Pallas kernels  86.8 us (91%)
  local copies, waits for them, and re-layouts  7.2 us (8%)
    pallas_call x1, Pallas kernels, per_device(): pl.pallas_call(functools.partial(kernel, ncl, nme, nx), out_shape=(out, o...  86.8 us
    unnamed x11, local copies, waits for them, and re-layouts  7.2 us

profile of v1, /device:TPU:1, one launch (start us, length us, event | category | flops | bytes accessed | tf_op | source)
XLA Modules:
  0.0 94.6 jit_solution(8283262955097342686)
XLA Ops:
  0.6 0.7 copy.16
  1.3 0.7 copy.15
  2.1 0.9 copy.14
  3.0 0.0 copy-start
  3.0 1.6 %copy-done = bf16[1,1,1024,1024]{3,2,1,0:T(8,128)(2,1)S(1)} copy-done((bf16[1,1,1024,1024]{3,2,1,0:T(8,128)(2,1)S(1)}, bf16[1,1,1024,1024]{3,2,1,0:T(8,128)(2,1)}, u32[]{:S(2)}) %copy-start) | copy-done | bytes 2097176
  4.6 0.0 copy-start.1
  4.6 1.0 %copy-done.1 = f32[1,1,1024,128]{3,2,1,0:T(8,128)S(1)} copy-done((f32[1,1,1024,128]{3,2,1,0:T(8,128)S(1)}, f32[1,1,1024,128]{3,2,1,0:T(8,128)}, u32[]{:S(2)}) %copy-start.1) | copy-done | bytes 524312
  5.6 0.0 copy-start.2
  5.6 0.7 copy-done.2
  6.3 86.8 %cg.1 = (f32[1024,128]{1,0:T(8,128)S(1)}, f32[1024,128]{1,0:T(8,128)S(1)}) custom-call(bf16[1024,1024]{1,0:T(8,128)(2,1)S(1)} %bitcast.14, f32[1024,128]{1,0:T(8,128)S(1)} %bitcast.17, f32[6,1024]{1,0:T(8,128)S(1)} %bitcast.19, f32[6,3072]{1,0:T(8,128)S(1)} %bitcast.18, f32[6,128]{1,0:T(8,128)S(1)} %bitcast.20, s32[4]{0:T(128)S(1)} %bitcast.21), custom_call_target="tpu_custom_call" | custom-call | tf_op jit(solution)/shard_map/cg/pallas_call | solution.py:298
  93.0 0.8 copy.19
  93.8 0.8 copy.20
Async XLA Ops:
  3.0 1.6 %copy-start = (bf16[1,1,1024,1024]{3,2,1,0:T(8,128)(2,1)S(1)}, bf16[1,1,1024,1024]{3,2,1,0:T(8,128)(2,1)}, u32[]{:S(2)}) copy-start(bf16[1,1,1024,1024]{3,2,1,0:T(8,128)(2,1)} %param.6) | copy-start | bytes 6291460
  4.6 1.0 %copy-start.1 = (f32[1,1,1024,128]{3,2,1,0:T(8,128)S(1)}, f32[1,1,1024,128]{3,2,1,0:T(8,128)}, u32[]{:S(2)}) copy-start(f32[1,1,1024,128]{3,2,1,0:T(8,128)} %param.7) | copy-start | bytes 1572868
  5.6 0.7 copy-start.2

commit v2 on v1

v2 whole, which is shorter than its diff:
```python
import functools

import jax
import jax.numpy as jnp
from jax import lax
from jax.experimental import pallas as pl
from jax.experimental.pallas import tpu as pltpu
from jax.sharding import PartitionSpec as P

CAP = 64
TOP = 4 * CAP
MESH = pl.DeviceIdType.MESH
F32 = jnp.float32
BF16 = jnp.bfloat16

STEPS = (
    (0, 0), (-1, 0), (1, 0), (0, -1), (0, 1),
    (-2, 0), (2, 0), (0, -2), (0, 2), (-1, -1), (-1, 1), (1, -1), (1, 1),
)


def slot_of(one, two=(0, 0)):
    return STEPS.index((one[0] + two[0], one[1] + two[1]))


def opposite(slot):
    return STEPS.index((-STEPS[slot][0], -STEPS[slot][1]))


def dot(a, b):
    return jnp.dot(a, b, preferred_element_type=F32)


def split(x):
    high = x.astype(BF16)
    return high, (x - high.astype(F32)).astype(BF16)


def far_first(t, n):
    return n // 2 + ((t % 2) * 2 - 1) * ((t + 1) // 2)


def kernel(
    ncl, nme, nx,
    ops_hbm, rhs_hbm, modes_hbm, rows_hbm, start_hbm, counts,
    m_ref, p_ref,
    ops, rhs, modes, rows, start,
    bb, bt, ft, pad, hs, hb, h2, k13,
    v_ref, r_ref, p0_ref, u0_ref, p1_ref, im_ref,
    s1_send, s1_buf, q_send, q_buf, f_send, f_buf,
    g_buf, t_buf, t_send, c_buf, sg_buf, st_buf, st_send,
    local_sem, s1_sems, h_sems, q_sems, f_sems, g_sems, t_sems, c_sems, sg_sems, st_sems,
):
    i, j = lax.axis_index("cluster"), lax.axis_index("member")
    nz = ncl // nx
    wide, cols = 8 * nme, 6 * nme
    slots = ops.shape[0]

    def at_step(slot):
        di, dj = STEPS[slot]
        return lax.rem(i + (di + ncl), ncl), lax.rem(j + (dj + nme), nme)

    def member_peer(t):
        return lax.rem(j + far_first(t, nme), nme)

    def cluster_peer(t):
        z = lax.rem(i // nx + far_first(t // nx, nz), nz)
        x = lax.rem(i % nx + far_first(t % nx, nx), nx)
        return z * nx + x

    def over_members(body):
        lax.fori_loop(0, nme - 1, lambda t, _: (body(member_peer(t)), 0)[1], 0, unroll=UNROLL)

    def over_cluster(body):
        lax.fori_loop(0, ncl - 1, lambda t, _: (body(cluster_peer(t)), 0)[1], 0, unroll=UNROLL)

    def send(src, dst, sems, device):
        pltpu.make_async_remote_copy(
            src, dst, sems.at[0], sems.at[1], device_id=device, device_id_type=MESH
        ).start()

    def wait(ref, sem):
        pltpu.make_async_copy(ref, ref, sem).wait()

    loads = [
        pltpu.make_async_copy(src, dst, local_sem.at[n])
        for n, (src, dst) in enumerate(
            ((modes_hbm, modes), (start_hbm, start), (rows_hbm, rows), (ops_hbm, ops), (rhs_hbm, rhs))
        )
    ]
    for load in loads:
        load.start()

    barrier = pltpu.get_barrier_semaphore()

    def greet(device):
        pl.semaphore_signal(barrier, inc=1, device_id=device, device_id_type=MESH)

    for slot in range(9, 13):
        greet(at_step(slot))
    over_cluster(lambda peer: greet((peer, j)))
    over_members(lambda peer: greet((i, peer)))

    first = [counts[0] * 0, counts[0], counts[0] + counts[1], counts[0] + counts[1] + counts[2]]
    in_faces = first[3] + counts[3]
    face_rows = lax.broadcasted_iota(jnp.int32, (CAP, 128), 0)
    tile_row = lax.broadcasted_iota(jnp.int32, (8, 128), 0)
    tile_lane = lax.broadcasted_iota(jnp.int32, (8, 128), 1)

    def face_of(ref, f):
        block = ref[pl.ds(first[f], CAP), :]
        return jnp.where(face_rows < counts[f], block, 0.0)

    loads[0].wait()
    loads[1].wait()
    modes8 = jnp.concatenate([modes[:, 0, :], jnp.zeros((2, slots), F32)], 0)
    start8 = jnp.concatenate([start[:, 0, :], jnp.zeros((2, 128), F32)], 0)
    for f in range(4):
        turned = pltpu.roll(modes8[:, 0:TOP], lax.rem(TOP - first[f], TOP), 1)[:, 0:128]
        s1_send[f, 0:8, :] = jnp.where(tile_lane < counts[f], turned, 0.0)
        s1_send[f, 8:16, :] = start8

    pl.semaphore_wait(barrier, ncl + nme + 2)
    for f in range(4):
        send(s1_send.at[f], s1_buf.at[f ^ 1], s1_sems, at_step(f + 1))

    loads[2].wait()
    spread = (
        lax.broadcasted_iota(jnp.int32, (cols, wide), 1)
        == (lax.broadcasted_iota(jnp.int32, (cols, wide), 0) // 6) * 8
        + lax.broadcasted_iota(jnp.int32, (cols, wide), 0) % 6
    ).astype(BF16)
    row_values = jnp.concatenate([rows[:, 0, :], jnp.zeros((2, cols * ncl), F32)], 0)
    high, low = split(
        jnp.concatenate([row_values[:, k * cols : (k + 1) * cols] for k in range(ncl)], 0)
    )
    hs[...] = (dot(high, spread) + dot(low, spread)).reshape(ncl, 8, wide)
    hb[i] = hs[i]
    over_cluster(lambda peer: send(hs.at[peer], hb.at[i], h_sems, (peer, j)))

    pad[...] = jnp.zeros_like(pad)
    g_buf[:, :, 6:8, :] = jnp.zeros((3, nme, 2, 128), F32)
    c_buf[:, :, 6:8, :] = jnp.zeros((3, 13, 2, 128), F32)

    def pack(lo, hi, across):
        high, low = split(across)
        high, low = high.astype(F32), low.astype(F32)
        none = jnp.zeros((8, hi - lo), F32)
        bt[0:48, lo:hi] = jnp.concatenate([high, none], 0).astype(BF16)
        bt[48:96, lo:hi] = jnp.concatenate([low, none], 0).astype(BF16)
        bb[lo:hi, :] = jnp.concatenate([high, high, low, none], 0).T.astype(BF16)

    def expand(coeffs, lo=0, hi=None):
        high, low = split(coeffs)
        return dot(bb[lo:hi, :], jnp.concatenate([high, low, high, jnp.zeros((8, 128), BF16)], 0))

    pack(TOP, slots, jnp.concatenate([modes8[:, TOP:], jnp.zeros((32, slots - TOP), F32)], 0))
    m_ref[TOP:, :] = expand(jnp.concatenate([start8, jnp.zeros((32, 128), F32)], 0), TOP)
    loads[3].wait()
    loads[4].wait()
    r_ref[...] = rhs[...] - dot(ops[:, TOP:], m_ref[TOP:, :].astype(BF16))

    wait(s1_buf, s1_sems.at[1])
    across = [modes8[:, 0:TOP]]
    for f in range(4):
        block = jnp.concatenate([s1_buf[f, 0:8, :], jnp.zeros((8, TOP - 128), F32)], 1)
        across.append(-pltpu.roll(block, first[f], 1))
    pack(0, TOP, jnp.concatenate(across, 0))

    def times(parts, field):
        high, low = split(field)
        both = dot(parts[...], high)
        return both[0:40] + both[48:88] + dot(parts[0:48, :], low)[0:40]

    def assemble(ref, k):
        wait(f_buf.at[k], f_sems.at[k, 1])
        for f in range(4):
            pad[f, TOP : TOP + CAP, :] = f_buf[k, f]
        top = ref[0:TOP, :]
        for f in range(4):
            top = top - pad[f, pl.ds(TOP - first[f], TOP), :]
        ref[0:TOP, :] = top

    def send_faces(ref, k):
        for f in range(4):
            f_send[k, f] = face_of(ref, f)
            send(f_send.at[k, f], f_buf.at[k, f ^ 1], f_sems.at[k], at_step(f + 1))

    def send_terms(terms, k):
        q_send[k] = terms[8:40].reshape(4, 8, 128)
        for f in range(4):
            send(q_send.at[k, f], q_buf.at[k, f ^ 1], q_sems.at[k], at_step(f + 1))
        return terms[0:8]

    def received_terms(k):
        wait(q_buf.at[k], q_sems.at[k, 1])
        return q_buf[k, 0] + q_buf[k, 1] + q_buf[k, 2] + q_buf[k, 3]

    def inner_rows(product):
        return jnp.sum(product, 0, keepdims=True)

    def weighted(field):
        top_rows = lax.broadcasted_iota(jnp.int32, (TOP, 128), 0)
        square = field * field
        return inner_rows(square) - 0.5 * inner_rows(
            jnp.where(top_rows < in_faces, square[0:TOP], 0.0)
        )

    def gather(k, tile):
        mine = g_buf.at[k, j, pl.ds(0, 6)]
        g_buf[k, j] = tile
        over_members(lambda peer: send(mine, mine, g_sems.at[k], (i, peer)))

    def scatter(k):
        wait(g_buf.at[k, 0 : nme - 1, pl.ds(0, 6)], g_sems.at[k, 1])
        g_high, g_low = split(g_buf[k].reshape(wide, 128))
        part = dot(h2[...], jnp.concatenate([g_high, g_high], 0)) + dot(h2[:, 0:wide], g_low)
        t_send[k] = part.reshape(ncl, 8, 128)
        t_buf[k, i] = t_send[k, i]
        over_cluster(
            lambda peer: send(
                t_send.at[k, peer, pl.ds(0, 6)], t_buf.at[k, i, pl.ds(0, 6)], t_sems.at[k], (peer, j)
            )
        )

    def share(k, around):
        wait(t_buf.at[k, 0 : ncl - 1, pl.ds(0, 6)], t_sems.at[k, 1])
        total = jnp.sum(t_buf[k], 0)
        c_buf[k, 0] = jnp.where(tile_row < 6, total, 0.0)
        mine = c_buf.at[k, 0, pl.ds(0, 6)]
        for slot in range(around - 1, 0, -1):
            send(mine, c_buf.at[k, opposite(slot), pl.ds(0, 6)], c_sems.at[k], at_step(slot))

    def shared(k, around):
        wait(c_buf.at[k, 1:around, pl.ds(0, 6)], c_sems.at[k, 1])

    def near(k):
        return c_buf[k, 0:5].reshape(40, 128)

    def coupled(k):
        high, low = split(c_buf[k].reshape(104, 128))
        fill = jnp.zeros((24, 128), BF16)
        high, low = jnp.concatenate([high, fill], 0), jnp.concatenate([low, fill], 0)
        both = dot(k13[...], high)
        return both[0:8] + both[8:16] + dot(k13[...], low)[0:8]

    def gather_sums(k, sums):
        sg_buf[k, j] = jnp.concatenate(sums, 0)
        mine = sg_buf.at[k, j]
        over_members(lambda peer: send(mine, mine, sg_sems.at[k], (i, peer)))

    def scatter_sums(k):
        wait(sg_buf.at[k, 0 : nme - 1], sg_sems.at[k, 1])
        total = jnp.sum(sg_buf[k], 0)
        st_send[k] = total
        st_buf[k, i] = total
        over_cluster(lambda peer: send(st_send.at[k], st_buf.at[k, i], st_sems.at[k], (peer, j)))

    def sums(k):
        wait(st_buf.at[k, 0 : ncl - 1], st_sems.at[k, 1])
        total = jnp.sum(st_buf[k], 0)
        return total[0:1], total[1:2], total[2:3]

    starts = jnp.concatenate([start8] + [s1_buf[f, 8:16, :] for f in range(4)], 0)
    m_ref[0:TOP, :] = expand(starts, 0, TOP)
    r_ref[...] = r_ref[...] - dot(ops[:, 0:TOP], m_ref[0:TOP, :].astype(BF16))
    own = send_terms(times(bt, r_ref[...]), 0)

    gather(0, own + received_terms(0))
    send_faces(r_ref, 0)

    both = dot(bt[...], ops[...])
    high, low = split(both[0:48] + both[48:96])
    ft[0:48, :] = high
    ft[48:96, :] = low
    both = dot(ft[...], bb[...])
    own_rows = send_terms(both[0:40] + both[48:88] + pltpu.roll(both[0:40], 48, 1), 1)
    assemble(r_ref, 0)
    gr_own = send_terms(times(ft, r_ref[...]), 2)
    wait(hb.at[0 : ncl - 1], h_sems.at[1])
    high, low = split(hb[...].reshape(8 * ncl, wide))
    h2[:, 0:wide] = high
    h2[:, wide : 2 * wide] = low
    scatter(0)
    wait(q_buf.at[1], q_sems.at[1, 1])
    around_rows = jnp.where(tile_lane < 40, own_rows, 0.0)
    for f in range(4):
        for n in range(5):
            slot = slot_of(STEPS[f + 1], STEPS[n])
            moved = q_buf[1, f]
            if slot != n:
                moved = pltpu.roll(moved, (8 * (slot - n)) % 128, 1)
            around_rows = around_rows + jnp.where(
                (tile_lane >= 8 * slot) & (tile_lane < 8 * slot + 8), moved, 0.0
            )
    high, low = split(around_rows)
    k13[...] = jnp.concatenate([high, low], 0)
    gr = gr_own + received_terms(2)
    share(0, 13)
    shared(0, 13)
    tile1 = gr - coupled(0)
    gather(1, tile1)

    p0_ref[...] = r_ref[...] - expand(near(0))
    u0_ref[...] = dot(ops[...], p0_ref[...].astype(BF16))
    send_faces(u0_ref, 1)
    gather_sums(
        0,
        [weighted(p0_ref[...]), inner_rows(p0_ref[...] * u0_ref[...]), jnp.zeros((1, 128), F32)],
    )
    scatter(1)
    im_ref[...] = u0_ref[...]
    assemble(im_ref, 1)
    gi_own = send_terms(times(ft, im_ref[...]), 3)
    scatter_sums(0)
    gi = gi_own + received_terms(3)
    share(1, 13)
    norm0, curv0, _ = sums(0)
    alpha0 = norm0 / curv0
    r_ref[...] = r_ref[...] - alpha0 * im_ref[...]
    shared(1, 13)
    gather(2, tile1 - alpha0 * (gi - coupled(1)))

    coeffs1 = near(0) - alpha0 * near(1)
    p1_ref[...] = r_ref[...] - expand(coeffs1)
    high, low = split(p1_ref[...])
    v_ref[...] = dot(ops[...], high) + dot(ops[...], low)
    send_faces(v_ref, 2)
    gather_sums(
        1,
        [
            weighted(p1_ref[...]),
            inner_rows(p1_ref[...] * v_ref[...]),
            inner_rows(p1_ref[...] * u0_ref[...] + p0_ref[...] * v_ref[...]),
        ],
    )
    scatter(2)
    scatter_sums(1)
    assemble(v_ref, 2)
    share(2, 5)
    norm1, curv1, cross = sums(1)
    beta = norm1 / norm0
    alpha1 = norm1 / (curv1 + beta * (cross + beta * curv0))
    m_ref[...] = m_ref[...] + (alpha0 + alpha1 * beta) * p0_ref[...] + alpha1 * p1_ref[...]
    r_ref[...] = r_ref[...] - alpha1 * (v_ref[...] + beta * im_ref[...])
    shared(2, 5)
    p_ref[...] = r_ref[...] - expand(coeffs1 - alpha1 * (near(2) + beta * near(1)))

    wait(s1_buf, s1_sems.at[0])
    wait(hb.at[0 : ncl - 1], h_sems.at[0])
    for k in range(4):
        wait(q_buf.at[k], q_sems.at[k, 0])
    for k in range(3):
        wait(f_buf.at[k], f_sems.at[k, 0])
        wait(g_buf.at[k, 0 : nme - 1, pl.ds(0, 6)], g_sems.at[k, 0])
        wait(t_buf.at[k, 0 : ncl - 1, pl.ds(0, 6)], t_sems.at[k, 0])
        wait(c_buf.at[k, 1 : (13, 13, 5)[k], pl.ds(0, 6)], c_sems.at[k, 0])
    for k in range(2):
        wait(sg_buf.at[k, 0 : nme - 1], sg_sems.at[k, 0])
        wait(st_buf.at[k, 0 : ncl - 1], st_sems.at[k, 0])


UNROLL = True
PIECES = 4


def finish(m_in, p_in, m_out, p_out, held, sems):
    size = m_in.shape[0] // PIECES
    pairs = [
        (src.at[pl.ds(n * size, size)], held.at[k, n], dst.at[pl.ds(n * size, size)], sems.at[0, k, n], sems.at[1, k, n])
        for k, (src, dst) in enumerate(((m_in, m_out), (p_in, p_out)))
        for n in range(PIECES)
    ]
    for src, here, _, sem, _ in pairs:
        pltpu.make_async_copy(src, here, sem).start()
    for src, here, dst, sem, sem2 in pairs:
        pltpu.make_async_copy(src, here, sem).wait()
        pltpu.make_async_copy(here, dst, sem2).start()
    for _, here, dst, _, sem2 in pairs:
        pltpu.make_async_copy(here, dst, sem2).wait()


def solution(mesh):
    ncl, nme = mesh.shape["cluster"], mesh.shape["member"]
    nx = 4 if ncl % 4 == 0 else 1

    def per_device(dual_ops, dual_rhs, rigid_modes, coarse_rows, start_coeffs, face_counts):
        slots, cases = dual_rhs.shape[2:]
        field = pltpu.VMEM((slots, cases), F32)
        out = jax.ShapeDtypeStruct((slots, cases), F32)

        def by_row(x):
            return x.reshape(x.shape[2], 1, x.shape[3])

        multipliers, projected = pl.pallas_call(
            functools.partial(kernel, ncl, nme, nx),
            out_shape=(out, out),
            in_specs=[pl.BlockSpec(memory_space=pltpu.HBM)] * 5
            + [pl.BlockSpec(memory_space=pltpu.SMEM)],
            out_specs=(pl.BlockSpec(memory_space=pltpu.VMEM),) * 2,
            scratch_shapes=[
                pltpu.VMEM((slots, slots), BF16),
                field,
                pltpu.VMEM((6, 1, slots), F32),
                pltpu.VMEM((6, 1, 6 * ncl * nme), F32),
                pltpu.VMEM((6, 1, cases), F32),
                pltpu.VMEM((slots, 128), BF16),
                pltpu.VMEM((96, slots), BF16),
                pltpu.VMEM((96, slots), BF16),
                pltpu.VMEM((4, 2 * TOP + CAP, cases), F32),
                pltpu.VMEM((ncl, 8, 8 * nme), F32),
                pltpu.VMEM((ncl, 8, 8 * nme), F32),
                pltpu.VMEM((8 * ncl, 16 * nme), BF16),
                pltpu.VMEM((16, 128), BF16),
                field, field, field, field, field, field,
                pltpu.VMEM((4, 16, cases), F32),
                pltpu.VMEM((4, 16, cases), F32),
                pltpu.VMEM((4, 4, 8, cases), F32),
                pltpu.VMEM((4, 4, 8, cases), F32),
                pltpu.VMEM((3, 4, CAP, cases), F32),
                pltpu.VMEM((3, 4, CAP, cases), F32),
                pltpu.VMEM((3, nme, 8, cases), F32),
                pltpu.VMEM((3, ncl, 8, cases), F32),
                pltpu.VMEM((3, ncl, 8, cases), F32),
                pltpu.VMEM((3, 13, 8, cases), F32),
                pltpu.VMEM((2, nme, 3, cases), F32),
                pltpu.VMEM((2, ncl, 3, cases), F32),
                pltpu.VMEM((2, 3, cases), F32),
                pltpu.SemaphoreType.DMA((5,)),
                pltpu.SemaphoreType.DMA((2,)),
                pltpu.SemaphoreType.DMA((2,)),
                pltpu.SemaphoreType.DMA((4, 2)),
                pltpu.SemaphoreType.DMA((3, 2)),
                pltpu.SemaphoreType.DMA((3, 2)),
                pltpu.SemaphoreType.DMA((3, 2)),
                pltpu.SemaphoreType.DMA((3, 2)),
                pltpu.SemaphoreType.DMA((2, 2)),
                pltpu.SemaphoreType.DMA((2, 2)),
            ],
            compiler_params=pltpu.CompilerParams(
                collective_id=0, has_side_effects=True, vmem_limit_bytes=60 << 20
            ),
            name="cg",
        )(
            dual_ops[0, 0], dual_rhs[0, 0], by_row(rigid_modes), by_row(coarse_rows),
            by_row(start_coeffs), face_counts[0, 0],
        )
        multipliers, projected = pl.pallas_call(
            finish,
            out_shape=(out, out),
            in_specs=[pl.BlockSpec(memory_space=pl.ANY)] * 2,
            out_specs=(pl.BlockSpec(memory_space=pl.ANY),) * 2,
            scratch_shapes=[pltpu.VMEM((2, PIECES, slots // PIECES, cases), F32), pltpu.SemaphoreType.DMA((2, 2, PIECES))],
            name="finish",
        )(multipliers, projected)
        return multipliers[None, None], projected[None, None]

    whole = P("cluster", "member", None, None)
    return jax.shard_map(
        per_device,
        mesh=mesh,
        in_specs=(whole,) * 5 + (P("cluster", "member", None),),
        out_specs=(whole, whole),
        check_vma=False,
    )
```

time: 95 us -> 75.8 us (0.80)
  Pallas kernels: 86.8 us -> 75 us
  local copies, waits for them, and re-layouts: 7.2 us -> 0 us
    pallas_call x1, Pallas kernels: 86.8 us -> 72.9 us  [per_device(): pl.pallas_call(functools.partial(kernel, ncl, nme, nx), out_shape=(out, o...]
    unnamed x11 -> x0, local copies, waits for them, and re-layouts: 7.2 us -> none
    pallas_call x0 -> x1, Pallas kernels: none -> 2.09 us  [per_device(): pl.pallas_call(finish, out_shape=(out, out), in_specs=[pl.BlockSpec(memor...]
where the time goes in v2:
time: 75.8 us; the launch traced here: 75.7 us
  Pallas kernels  75 us (99%)
    pallas_call x1, Pallas kernels, per_device(): pl.pallas_call(functools.partial(kernel, ncl, nme, nx), out_shape=(out, o...  72.9 us
    pallas_call x1, Pallas kernels, per_device(): pl.pallas_call(finish, out_shape=(out, out), in_specs=[pl.BlockSpec(memor...  2.09 us

profile of v2, /device:TPU:1, one launch (start us, length us, event | category | flops | bytes accessed | tf_op | source)
XLA Modules:
  0.0 75.7 jit_solution(4558616711553825244)
XLA Ops:
  0.6 72.9 %cg.1 = (f32[1024,128]{1,0:T(8,128)}, f32[1024,128]{1,0:T(8,128)}) custom-call(bf16[1024,1024]{1,0:T(8,128)(2,1)} %bitcast.8, f32[1024,128]{1,0:T(8,128)} %bitcast.9, f32[6,1,1024]{2,1,0:T(1,128)} %bitcast.11, f32[6,1,3072]{2,1,0:T(1,128)} %bitcast.10, f32[6,1,128]{2,1,0:T(1,128)} %bitcast.12, s32[4]{0:T(128)} %bitcast.13), custom_call_target="tpu_custom_call" | custom-call | tf_op jit(solution)/shard_map/cg/pallas_call | solution.py:395
  73.6 2.1 %finish.1 = (f32[1024,128]{1,0:T(8,128)}, f32[1024,128]{1,0:T(8,128)}) custom-call(f32[1024,128]{1,0:T(8,128)} %get-tuple-element.6.m_in, f32[1024,128]{1,0:T(8,128)} %get-tuple-element.7.p_in), custom_call_target="tpu_custom_call" | custom-call | tf_op jit(solution)/shard_map/finish/pallas_call | solution.py:448

commit v3 on v2

--- a/solution.py
+++ b/solution.py
@@ -15,12 +15,7 @@
 
 STEPS = (
     (0, 0), (-1, 0), (1, 0), (0, -1), (0, 1),
-    (-2, 0), (2, 0), (0, -2), (0, 2), (-1, -1), (-1, 1), (1, -1), (1, 1),
 )
-
-
-def slot_of(one, two=(0, 0)):
-    return STEPS.index((one[0] + two[0], one[1] + two[1]))
 
 
 def opposite(slot):
@@ -43,13 +38,14 @@
 def kernel(
     ncl, nme, nx,
     ops_hbm, rhs_hbm, modes_hbm, rows_hbm, start_hbm, counts,
-    m_ref, p_ref,
-    ops, rhs, modes, rows, start,
-    bb, bt, ft, pad, hs, hb, h2, k13,
-    v_ref, r_ref, p0_ref, u0_ref, p1_ref, im_ref,
+    m_hbm, p_hbm,
+    m_ref, p_ref, ops, rhs, modes, rows, start,
+    bb, bt, ft, pad, hs, hb, h2, m2, h_near, a_high, a_low, d_high, d_low, v_send, v_buf,
+    v_ref, r_ref, p0_ref, u0_ref, q_ref, im_ref,
     s1_send, s1_buf, q_send, q_buf, f_send, f_buf,
-    g_buf, t_buf, t_send, c_buf, sg_buf, st_buf, st_send,
-    local_sem, s1_sems, h_sems, q_sems, f_sems, g_sems, t_sems, c_sems, sg_sems, st_sems,
+    g_buf, e_buf, x_buf, t_buf, t_send, c_buf, sg_buf, st_buf, st_send,
+    local_sem, s1_sems, h_sems, q_sems, f_sems, g_sems, e_sems, x_sems, near_sems, v_sems,
+    t_sems, c_sems, sg_sems, st_sems,
 ):
     i, j = lax.axis_index("cluster"), lax.axis_index("member")
     nz = ncl // nx
@@ -78,6 +74,9 @@
         pltpu.make_async_remote_copy(
             src, dst, sems.at[0], sems.at[1], device_id=device, device_id_type=MESH
         ).start()
+
+    def store(n, src, dst, lo, hi):
+        return pltpu.make_async_copy(src.at[lo:hi], dst.at[lo:hi], local_sem.at[5 + n])
 
     def wait(ref, sem):
         pltpu.make_async_copy(ref, ref, sem).wait()
@@ -96,8 +95,6 @@
     def greet(device):
         pl.semaphore_signal(barrier, inc=1, device_id=device, device_id_type=MESH)
 
-    for slot in range(9, 13):
-        greet(at_step(slot))
     over_cluster(lambda peer: greet((peer, j)))
     over_members(lambda peer: greet((i, peer)))
 
@@ -120,7 +117,7 @@
         s1_send[f, 0:8, :] = jnp.where(tile_lane < counts[f], turned, 0.0)
         s1_send[f, 8:16, :] = start8
 
-    pl.semaphore_wait(barrier, ncl + nme + 2)
+    pl.semaphore_wait(barrier, ncl + nme - 2)
     for f in range(4):
         send(s1_send.at[f], s1_buf.at[f ^ 1], s1_sems, at_step(f + 1))
 
@@ -140,7 +137,8 @@
 
     pad[...] = jnp.zeros_like(pad)
     g_buf[:, :, 6:8, :] = jnp.zeros((3, nme, 2, 128), F32)
-    c_buf[:, :, 6:8, :] = jnp.zeros((3, 13, 2, 128), F32)
+    e_buf[:, :, 6:8, :] = jnp.zeros((2, nme, 2, 128), F32)
+    c_buf[:, :, 6:8, :] = jnp.zeros((3, 5, 2, 128), F32)
 
     def pack(lo, hi, across):
         high, low = split(across)
@@ -206,15 +204,25 @@
             jnp.where(top_rows < in_faces, square[0:TOP], 0.0)
         )
 
-    def gather(k, tile):
-        mine = g_buf.at[k, j, pl.ds(0, 6)]
-        g_buf[k, j] = tile
-        over_members(lambda peer: send(mine, mine, g_sems.at[k], (i, peer)))
+    def gather(buf, sems, k, tile):
+        mine = buf.at[k, j, pl.ds(0, 6)]
+        buf[k, j] = tile
+        over_members(lambda peer: send(mine, mine, sems.at[k], (i, peer)))
+
+    def gathered(buf, sems, k):
+        wait(buf.at[k, 0 : nme - 1, pl.ds(0, 6)], sems.at[k, 1])
+        return split(buf[k].reshape(wide, 128))
+
+    def two_part(matrix, parts):
+        high, low = parts
+        return dot(matrix[...], jnp.concatenate([high, high], 0)) + dot(matrix[:, 0:wide], low)
 
     def scatter(k):
-        wait(g_buf.at[k, 0 : nme - 1, pl.ds(0, 6)], g_sems.at[k, 1])
-        g_high, g_low = split(g_buf[k].reshape(wide, 128))
-        part = dot(h2[...], jnp.concatenate([g_high, g_high], 0)) + dot(h2[:, 0:wide], g_low)
+        if k == 0:
+            part = two_part(h2, gathered(g_buf, g_sems, 0))
+        else:
+            base = two_part(h2, gathered(e_buf, e_sems, k - 1))
+            part = base - two_part(m2, gathered(g_buf, g_sems, k))
         t_send[k] = part.reshape(ncl, 8, 128)
         t_buf[k, i] = t_send[k, i]
         over_cluster(
@@ -223,50 +231,35 @@
             )
         )
 
-    def share(k, around):
+    def share(k):
         wait(t_buf.at[k, 0 : ncl - 1, pl.ds(0, 6)], t_sems.at[k, 1])
-        total = jnp.sum(t_buf[k], 0)
-        c_buf[k, 0] = jnp.where(tile_row < 6, total, 0.0)
+        tile = jnp.where(tile_row < 6, jnp.sum(t_buf[k], 0), 0.0)
+        c_buf[k, 0] = tile
         mine = c_buf.at[k, 0, pl.ds(0, 6)]
-        for slot in range(around - 1, 0, -1):
+        for slot in range(1, 5):
             send(mine, c_buf.at[k, opposite(slot), pl.ds(0, 6)], c_sems.at[k], at_step(slot))
-
-    def shared(k, around):
-        wait(c_buf.at[k, 1:around, pl.ds(0, 6)], c_sems.at[k, 1])
+        if k < 2:
+            gather(g_buf, g_sems, k + 1, tile)
+
+    def alone(k):
+        return jnp.concatenate([c_buf[k, 0], jnp.zeros((32, 128), F32)], 0)
 
     def near(k):
-        return c_buf[k, 0:5].reshape(40, 128)
-
-    def coupled(k):
-        high, low = split(c_buf[k].reshape(104, 128))
-        fill = jnp.zeros((24, 128), BF16)
-        high, low = jnp.concatenate([high, fill], 0), jnp.concatenate([low, fill], 0)
-        both = dot(k13[...], high)
-        return both[0:8] + both[8:16] + dot(k13[...], low)[0:8]
-
-    def gather_sums(k, sums):
-        sg_buf[k, j] = jnp.concatenate(sums, 0)
-        mine = sg_buf.at[k, j]
-        over_members(lambda peer: send(mine, mine, sg_sems.at[k], (i, peer)))
-
-    def scatter_sums(k):
-        wait(sg_buf.at[k, 0 : nme - 1], sg_sems.at[k, 1])
-        total = jnp.sum(sg_buf[k], 0)
-        st_send[k] = total
-        st_buf[k, i] = total
-        over_cluster(lambda peer: send(st_send.at[k], st_buf.at[k, i], st_sems.at[k], (peer, j)))
-
-    def sums(k):
-        wait(st_buf.at[k, 0 : ncl - 1], st_sems.at[k, 1])
-        total = jnp.sum(st_buf[k], 0)
-        return total[0:1], total[1:2], total[2:3]
+        wait(c_buf.at[k, 1:5, pl.ds(0, 6)], c_sems.at[k, 1])
+        return c_buf[k].reshape(40, 128)
+
+    def apply(out, field, columns):
+        both = dot(ops[:, columns], jnp.concatenate(split(field[columns, :]), 1))
+        return out + both[:, 0:128] + both[:, 128:256]
+
+    upper, lower = slice(0, TOP), slice(TOP, slots)
 
     starts = jnp.concatenate([start8] + [s1_buf[f, 8:16, :] for f in range(4)], 0)
     m_ref[0:TOP, :] = expand(starts, 0, TOP)
     r_ref[...] = r_ref[...] - dot(ops[:, 0:TOP], m_ref[0:TOP, :].astype(BF16))
     own = send_terms(times(bt, r_ref[...]), 0)
 
-    gather(0, own + received_terms(0))
+    gather(g_buf, g_sems, 0, own + received_terms(0))
     send_faces(r_ref, 0)
 
     both = dot(bt[...], ops[...])
@@ -274,90 +267,149 @@
     ft[0:48, :] = high
     ft[48:96, :] = low
     both = dot(ft[...], bb[...])
-    own_rows = send_terms(both[0:40] + both[48:88] + pltpu.roll(both[0:40], 48, 1), 1)
-    assemble(r_ref, 0)
-    gr_own = send_terms(times(ft, r_ref[...]), 2)
+    x = both[0:40] + both[48:88] + pltpu.roll(both[0:40], 48, 1)
+    x = jnp.where(lax.broadcasted_iota(jnp.int32, (40, 128), 1) < 40, x, 0.0)
+    mine = x_buf.at[j]
+    x_buf[j] = (
+        x[0:16]
+        + pltpu.roll(x[16:32], 40, 1)
+        + pltpu.roll(jnp.concatenate([x[32:40], jnp.zeros((8, 128), F32)], 0), 80, 1)
+    )
+    over_members(lambda peer: send(mine, mine, x_sems, (i, peer)))
+
     wait(hb.at[0 : ncl - 1], h_sems.at[1])
     high, low = split(hb[...].reshape(8 * ncl, wide))
     h2[:, 0:wide] = high
     h2[:, wide : 2 * wide] = low
+    assemble(r_ref, 0)
+    gr_own = send_terms(times(ft, r_ref[...]), 1)
     scatter(0)
-    wait(q_buf.at[1], q_sems.at[1, 1])
-    around_rows = jnp.where(tile_lane < 40, own_rows, 0.0)
-    for f in range(4):
-        for n in range(5):
-            slot = slot_of(STEPS[f + 1], STEPS[n])
-            moved = q_buf[1, f]
-            if slot != n:
-                moved = pltpu.roll(moved, (8 * (slot - n)) % 128, 1)
-            around_rows = around_rows + jnp.where(
-                (tile_lane >= 8 * slot) & (tile_lane < 8 * slot + 8), moved, 0.0
-            )
-    high, low = split(around_rows)
-    k13[...] = jnp.concatenate([high, low], 0)
-    gr = gr_own + received_terms(2)
-    share(0, 13)
-    shared(0, 13)
-    tile1 = gr - coupled(0)
-    gather(1, tile1)
-
-    p0_ref[...] = r_ref[...] - expand(near(0))
-    u0_ref[...] = dot(ops[...], p0_ref[...].astype(BF16))
+    for n, step in enumerate((2, 1)):
+        send(hb.at[:, pl.ds(0, 6)], h_near.at[n, :, pl.ds(0, 6)], near_sems.at[n], at_step(step))
+    gather(e_buf, e_sems, 0, gr_own + received_terms(1))
+
+    wait(x_buf.at[0 : nme - 1], x_sems.at[1])
+    lanes = 5 * wide
+    q_row = lax.broadcasted_iota(jnp.int32, (128, lanes), 0)
+    q_lane = lax.broadcasted_iota(jnp.int32, (128, lanes), 1)
+    source = (q_lane // wide) * 8 + q_lane % 8
+    for n in range(5):
+        q = (q_row == source + 40 * (n // 2)).astype(BF16)
+        half = 8 * (n % 2)
+        high, low = split(x_buf[:, half : half + 8, :].reshape(wide, 128))
+        d_row = lax.broadcasted_iota(jnp.int32, (wide, lanes), 0)
+        d_lane = lax.broadcasted_iota(jnp.int32, (wide, lanes), 1)
+        same = d_row // 8 == (d_lane % wide) // 8
+        d_high[n * wide : (n + 1) * wide, :] = jnp.where(same, dot(high, q), 0.0).astype(BF16)
+        d_low[n * wide : (n + 1) * wide, :] = jnp.where(same, dot(low, q), 0.0).astype(BF16)
+    share(0)
+    for n in range(2):
+        wait(h_near.at[n, :, pl.ds(0, 6)], near_sems.at[n, 1])
+    mid = hb[...].reshape(8 * ncl, wide)
+    groups = [mid] + [h_near[n].reshape(8 * ncl, wide) for n in range(2)]
+    groups += [pltpu.roll(mid, 8, 1), pltpu.roll(mid, wide - 8, 1)]
+    for n, group in enumerate(groups):
+        high, low = split(group)
+        a_high[:, n * wide : (n + 1) * wide] = high
+        a_low[:, n * wide : (n + 1) * wide] = low
+
+    def group_of(n):
+        at = slice(n * wide, (n + 1) * wide)
+        return (
+            dot(a_high[...], d_high[:, at]) + dot(a_high[...], d_low[:, at]) + dot(a_low[...], d_high[:, at])
+        )
+
+    for n in range(2):
+        v_send[n] = group_of(n + 1).reshape(ncl, 8, wide)
+        send(
+            v_send.at[n, :, pl.ds(0, 6)], v_buf.at[n, :, pl.ds(0, 6)], v_sems.at[n], at_step(n + 1)
+        )
+    v_ref[0 : 8 * ncl, 0:wide] = (
+        group_of(0) + pltpu.roll(group_of(3), wide - 8, 1) + pltpu.roll(group_of(4), 8, 1)
+    )
+
+    p0_ref[lower, :] = r_ref[lower, :] - expand(alone(0), TOP)
+    u0_ref[...] = apply(0.0, p0_ref, lower)
+    p0_ref[upper, :] = r_ref[upper, :] - expand(near(0), 0, TOP)
+    u0_ref[...] = apply(u0_ref[...], p0_ref, upper)
     send_faces(u0_ref, 1)
-    gather_sums(
-        0,
-        [weighted(p0_ref[...]), inner_rows(p0_ref[...] * u0_ref[...]), jnp.zeros((1, 128), F32)],
+    for n in range(2):
+        wait(v_buf.at[n, :, pl.ds(0, 6)], v_sems.at[n, 1])
+    high, low = split(
+        v_ref[0 : 8 * ncl, 0:wide]
+        + v_buf[0].reshape(8 * ncl, wide)
+        + v_buf[1].reshape(8 * ncl, wide)
     )
+    m2[:, 0:wide] = high
+    m2[:, wide : 2 * wide] = low
     scatter(1)
     im_ref[...] = u0_ref[...]
     assemble(im_ref, 1)
-    gi_own = send_terms(times(ft, im_ref[...]), 3)
-    scatter_sums(0)
-    gi = gi_own + received_terms(3)
-    share(1, 13)
-    norm0, curv0, _ = sums(0)
+    gi_own = send_terms(times(ft, im_ref[...]), 2)
+    sum_rows = [weighted(p0_ref[...]), inner_rows(p0_ref[...] * u0_ref[...])]
+    gather(e_buf, e_sems, 1, gi_own + received_terms(2))
+    share(1)
+
+    q_ref[lower, :] = im_ref[lower, :] - expand(alone(1), TOP)
+    v_ref[...] = apply(0.0, q_ref, lower)
+    q_ref[upper, :] = im_ref[upper, :] - expand(near(1), 0, TOP)
+    v_ref[...] = apply(v_ref[...], q_ref, upper)
+    sum_rows += [
+        weighted(q_ref[...]),
+        inner_rows(q_ref[...] * v_ref[...]),
+        inner_rows(p0_ref[...] * v_ref[...] + q_ref[...] * u0_ref[...]),
+    ]
+    in_face = lax.broadcasted_iota(jnp.int32, (TOP, 128), 0) < in_faces
+    cross = p0_ref[...] * q_ref[...]
+    sum_rows.append(inner_rows(cross) - 0.5 * inner_rows(jnp.where(in_face, cross[upper], 0.0)))
+    sg_buf[j] = jnp.concatenate(sum_rows, 0)
+    mine = sg_buf.at[j]
+    over_members(lambda peer: send(mine, mine, sg_sems, (i, peer)))
+    send_faces(v_ref, 2)
+    scatter(2)
+    wait(sg_buf.at[0 : nme - 1], sg_sems.at[1])
+    st_send[...] = jnp.sum(sg_buf[...], 0)
+    st_buf[i] = st_send[...]
+    over_cluster(lambda peer: send(st_send, st_buf.at[i], st_sems, (peer, j)))
+    assemble(v_ref, 2)
+    share(2)
+    v_ref[lower, :] = v_ref[lower, :] - expand(alone(2), TOP)
+    wait(st_buf.at[0 : ncl - 1], st_sems.at[1])
+    total = jnp.sum(st_buf[...], 0)
+    norm0, curv0, norm_q, curv_q, curv_pq, norm_pq = [total[n : n + 1] for n in range(6)]
     alpha0 = norm0 / curv0
-    r_ref[...] = r_ref[...] - alpha0 * im_ref[...]
-    shared(1, 13)
-    gather(2, tile1 - alpha0 * (gi - coupled(1)))
-
-    coeffs1 = near(0) - alpha0 * near(1)
-    p1_ref[...] = r_ref[...] - expand(coeffs1)
-    high, low = split(p1_ref[...])
-    v_ref[...] = dot(ops[...], high) + dot(ops[...], low)
-    send_faces(v_ref, 2)
-    gather_sums(
-        1,
-        [
-            weighted(p1_ref[...]),
-            inner_rows(p1_ref[...] * v_ref[...]),
-            inner_rows(p1_ref[...] * u0_ref[...] + p0_ref[...] * v_ref[...]),
-        ],
-    )
-    scatter(2)
-    scatter_sums(1)
-    assemble(v_ref, 2)
-    share(2, 5)
-    norm1, curv1, cross = sums(1)
+    norm1 = norm0 - alpha0 * (2.0 * norm_pq - alpha0 * norm_q)
     beta = norm1 / norm0
-    alpha1 = norm1 / (curv1 + beta * (cross + beta * curv0))
-    m_ref[...] = m_ref[...] + (alpha0 + alpha1 * beta) * p0_ref[...] + alpha1 * p1_ref[...]
-    r_ref[...] = r_ref[...] - alpha1 * (v_ref[...] + beta * im_ref[...])
-    shared(2, 5)
-    p_ref[...] = r_ref[...] - expand(coeffs1 - alpha1 * (near(2) + beta * near(1)))
-
+    scale = 1.0 + beta
+    alpha1 = norm1 / (scale * (scale * curv0 - alpha0 * curv_pq) + alpha0 * alpha0 * curv_q)
+    first_by = alpha0 + alpha1 * scale
+    second_by = alpha0 * alpha1
+    m_ref[...] = m_ref[...] + first_by * p0_ref[...] - second_by * q_ref[...]
+    store(0, m_ref, m_hbm, 0, slots).start()
+    p_ref[lower, :] = p0_ref[lower, :] - first_by * q_ref[lower, :] + second_by * v_ref[lower, :]
+    store(1, p_ref, p_hbm, TOP, slots).start()
+    last = p0_ref[upper, :] - first_by * q_ref[upper, :] + second_by * v_ref[upper, :]
+    p_ref[upper, :] = last - second_by * expand(near(2), 0, TOP)
+    store(2, p_ref, p_hbm, 0, TOP).start()
+
+    store(0, m_ref, m_hbm, 0, slots).wait()
+    store(1, p_ref, p_hbm, TOP, slots).wait()
+    store(2, p_ref, p_hbm, 0, TOP).wait()
     wait(s1_buf, s1_sems.at[0])
     wait(hb.at[0 : ncl - 1], h_sems.at[0])
-    for k in range(4):
+    wait(x_buf.at[0 : nme - 1], x_sems.at[0])
+    for n in range(2):
+        wait(h_near.at[n, :, pl.ds(0, 6)], near_sems.at[n, 0])
+        wait(v_buf.at[n, :, pl.ds(0, 6)], v_sems.at[n, 0])
+        wait(e_buf.at[n, 0 : nme - 1, pl.ds(0, 6)], e_sems.at[n, 0])
+    for k in range(3):
         wait(q_buf.at[k], q_sems.at[k, 0])
-    for k in range(3):
         wait(f_buf.at[k], f_sems.at[k, 0])
         wait(g_buf.at[k, 0 : nme - 1, pl.ds(0, 6)], g_sems.at[k, 0])
         wait(t_buf.at[k, 0 : ncl - 1, pl.ds(0, 6)], t_sems.at[k, 0])
-        wait(c_buf.at[k, 1 : (13, 13, 5)[k], pl.ds(0, 6)], c_sems.at[k, 0])
-    for k in range(2):
-        wait(sg_buf.at[k, 0 : nme - 1], sg_sems.at[k, 0])
-        wait(st_buf.at[k, 0 : ncl - 1], st_sems.at[k, 0])
+        wait(c_buf.at[k, 1:5, pl.ds(0, 6)], c_sems.at[k, 0])
+    wait(sg_buf.at[0 : nme - 1], sg_sems.at[0])
+    wait(st_buf.at[0 : ncl - 1], st_sems.at[0])
 
 
 UNROLL = True
@@ -397,8 +449,9 @@
             out_shape=(out, out),
             in_specs=[pl.BlockSpec(memory_space=pltpu.HBM)] * 5
             + [pl.BlockSpec(memory_space=pltpu.SMEM)],
-            out_specs=(pl.BlockSpec(memory_space=pltpu.VMEM),) * 2,
+            out_specs=(pl.BlockSpec(memory_space=pl.ANY),) * 2,
             scratch_shapes=[
+                field, field,
                 pltpu.VMEM((slots, slots), BF16),
                 field,
                 pltpu.VMEM((6, 1, slots), F32),
@@ -411,31 +464,44 @@
                 pltpu.VMEM((ncl, 8, 8 * nme), F32),
                 pltpu.VMEM((ncl, 8, 8 * nme), F32),
                 pltpu.VMEM((8 * ncl, 16 * nme), BF16),
-                pltpu.VMEM((16, 128), BF16),
+                pltpu.VMEM((8 * ncl, 16 * nme), BF16),
+                pltpu.VMEM((2, ncl, 8, 8 * nme), F32),
+                pltpu.VMEM((8 * ncl, 40 * nme), BF16),
+                pltpu.VMEM((8 * ncl, 40 * nme), BF16),
+                pltpu.VMEM((40 * nme, 40 * nme), BF16),
+                pltpu.VMEM((40 * nme, 40 * nme), BF16),
+                pltpu.VMEM((2, ncl, 8, 8 * nme), F32),
+                pltpu.VMEM((2, ncl, 8, 8 * nme), F32),
                 field, field, field, field, field, field,
                 pltpu.VMEM((4, 16, cases), F32),
                 pltpu.VMEM((4, 16, cases), F32),
-                pltpu.VMEM((4, 4, 8, cases), F32),
-                pltpu.VMEM((4, 4, 8, cases), F32),
+                pltpu.VMEM((3, 4, 8, cases), F32),
+                pltpu.VMEM((3, 4, 8, cases), F32),
                 pltpu.VMEM((3, 4, CAP, cases), F32),
                 pltpu.VMEM((3, 4, CAP, cases), F32),
                 pltpu.VMEM((3, nme, 8, cases), F32),
+                pltpu.VMEM((2, nme, 8, cases), F32),
+                pltpu.VMEM((nme, 16, 128), F32),
                 pltpu.VMEM((3, ncl, 8, cases), F32),
                 pltpu.VMEM((3, ncl, 8, cases), F32),
-                pltpu.VMEM((3, 13, 8, cases), F32),
-                pltpu.VMEM((2, nme, 3, cases), F32),
-                pltpu.VMEM((2, ncl, 3, cases), F32),
-                pltpu.VMEM((2, 3, cases), F32),
-                pltpu.SemaphoreType.DMA((5,)),
+                pltpu.VMEM((3, 5, 8, cases), F32),
+                pltpu.VMEM((nme, 6, cases), F32),
+                pltpu.VMEM((ncl, 6, cases), F32),
+                pltpu.VMEM((6, cases), F32),
+                pltpu.SemaphoreType.DMA((8,)),
                 pltpu.SemaphoreType.DMA((2,)),
                 pltpu.SemaphoreType.DMA((2,)),
-                pltpu.SemaphoreType.DMA((4, 2)),
-                pltpu.SemaphoreType.DMA((3, 2)),
                 pltpu.SemaphoreType.DMA((3, 2)),
                 pltpu.SemaphoreType.DMA((3, 2)),
                 pltpu.SemaphoreType.DMA((3, 2)),
                 pltpu.SemaphoreType.DMA((2, 2)),
+                pltpu.SemaphoreType.DMA((2,)),
                 pltpu.SemaphoreType.DMA((2, 2)),
+                pltpu.SemaphoreType.DMA((2, 2)),
+                pltpu.SemaphoreType.DMA((3, 2)),
+                pltpu.SemaphoreType.DMA((3, 2)),
+                pltpu.SemaphoreType.DMA((2,)),
+                pltpu.SemaphoreType.DMA((2,)),
             ],
             compiler_params=pltpu.CompilerParams(
                 collective_id=0, has_side_effects=True, vmem_limit_bytes=60 << 20

time: 75.8 us -> 70.3 us (0.927)
  Pallas kernels: 75 us -> 69.5 us
    pallas_call x1, Pallas kernels: 72.9 us -> 67.4 us  [per_device(): pl.pallas_call(functools.partial(kernel, ncl, nme, nx), out_shape=(out, o...]
where the time goes in v3:
time: 70.3 us; the launch traced here: 70.1 us
  Pallas kernels  69.5 us (99%)
    pallas_call x1, Pallas kernels, per_device(): pl.pallas_call(functools.partial(kernel, ncl, nme, nx), out_shape=(out, o...  67.4 us
    pallas_call x1, Pallas kernels, per_device(): pl.pallas_call(finish, out_shape=(out, out), in_specs=[pl.BlockSpec(memor...  2.09 us

profile of v3, /device:TPU:1, one launch (start us, length us, event | category | flops | bytes accessed | tf_op | source)
XLA Modules:
  0.0 70.1 jit_solution(17840105484345403689)
XLA Ops:
  0.6 67.4 %cg.1 = (f32[1024,128]{1,0:T(8,128)}, f32[1024,128]{1,0:T(8,128)}) custom-call(bf16[1024,1024]{1,0:T(8,128)(2,1)} %bitcast.8, f32[1024,128]{1,0:T(8,128)} %bitcast.9, f32[6,1,1024]{2,1,0:T(1,128)} %bitcast.11, f32[6,1,3072]{2,1,0:T(1,128)} %bitcast.10, f32[6,1,128]{2,1,0:T(1,128)} %bitcast.12, s32[4]{0:T(128)} %bitcast.13), custom_call_target="tpu_custom_call" | custom-call | tf_op jit(solution)/shard_map/cg/pallas_call | solution.py:447
  68.1 2.1 %finish.1 = (f32[1024,128]{1,0:T(8,128)}, f32[1024,128]{1,0:T(8,128)}) custom-call(f32[1024,128]{1,0:T(8,128)} %get-tuple-element.6.m_in, f32[1024,128]{1,0:T(8,128)} %get-tuple-element.7.p_in), custom_call_target="tpu_custom_call" | custom-call | tf_op jit(solution)/shard_map/finish/pallas_call | solution.py:514

commit v4 on v3

--- a/solution.py
+++ b/solution.py
@@ -44,7 +44,7 @@
     v_ref, r_ref, p0_ref, u0_ref, q_ref, im_ref,
     s1_send, s1_buf, q_send, q_buf, f_send, f_buf,
     g_buf, e_buf, x_buf, t_buf, t_send, c_buf, sg_buf, st_buf, st_send,
-    local_sem, s1_sems, h_sems, q_sems, f_sems, g_sems, e_sems, x_sems, near_sems, v_sems,
+    news, local_sem, s1_sems, h_sems, q_sems, f_sems, g_sems, e_sems, x_sems, near_sems, v_sems,
     t_sems, c_sems, sg_sems, st_sems,
 ):
     i, j = lax.axis_index("cluster"), lax.axis_index("member")
@@ -95,8 +95,39 @@
     def greet(device):
         pl.semaphore_signal(barrier, inc=1, device_id=device, device_id_type=MESH)
 
-    over_cluster(lambda peer: greet((peer, j)))
-    over_members(lambda peer: greet((i, peer)))
+    ny, z, x, y, core = nme // 2, i // nx, i % nx, j // 2, j % 2
+    assert nz <= 8 and ny <= 8 and nx in (1, 4)
+
+    def along(axis, step):
+        if axis == "z":
+            return lax.rem(z + (step + nz), nz) * nx + x, j
+        if axis == "x":
+            return z * nx + lax.rem(x + (step + nx), nx), j
+        return i, lax.rem(y + (step + ny), ny) * 2 + core
+
+    def both_ways(distance, over):
+        sizes = (("z", nz), ("y", ny), ("x", nx))
+        return [
+            along(axis, step) for axis, n in sizes if n > over for step in (-distance, distance)
+        ]
+
+    other_core = (i, y * 2 + 1 - core)
+    beside = [at_step(slot) for slot in range(1, 5)] + both_ways(1, 1) + [other_core]
+    rounds = (
+        both_ways(1, 2),
+        [along(axis, step) for axis, n in (("z", nz), ("y", ny)) if n > 4 for step in (-2, 2)],
+        ([along("x", step) for step in (-1, 1, 2)] if nx > 1 else []) + [other_core],
+    )
+    for device in beside:
+        greet(device)
+
+    def tell(n):
+        for device in rounds[n]:
+            pl.semaphore_signal(news.at[n], inc=1, device_id=device, device_id_type=MESH)
+
+    def hear(n):
+        if rounds[n]:
+            pl.semaphore_wait(news.at[n], len(rounds[n]))
 
     first = [counts[0] * 0, counts[0], counts[0] + counts[1], counts[0] + counts[1] + counts[2]]
     in_faces = first[3] + counts[3]
@@ -117,9 +148,36 @@
         s1_send[f, 0:8, :] = jnp.where(tile_lane < counts[f], turned, 0.0)
         s1_send[f, 8:16, :] = start8
 
-    pl.semaphore_wait(barrier, ncl + nme - 2)
+    pl.semaphore_wait(barrier, len(beside))
     for f in range(4):
         send(s1_send.at[f], s1_buf.at[f ^ 1], s1_sems, at_step(f + 1))
+    tell(0)
+
+    pad[...] = jnp.zeros_like(pad)
+    g_buf[:, :, 6:8, :] = jnp.zeros((3, nme, 2, 128), F32)
+    e_buf[:, :, 6:8, :] = jnp.zeros((2, nme, 2, 128), F32)
+    c_buf[:, :, 6:8, :] = jnp.zeros((3, 5, 2, 128), F32)
+
+    def pack(lo, hi, across):
+        high, low = split(across)
+        high, low = high.astype(F32), low.astype(F32)
+        none = jnp.zeros((8, hi - lo), F32)
+        bt[0:48, lo:hi] = jnp.concatenate([high, none], 0).astype(BF16)
+        bt[48:96, lo:hi] = jnp.concatenate([low, none], 0).astype(BF16)
+        bb[lo:hi, :] = jnp.concatenate([high, high, low, none], 0).T.astype(BF16)
+
+    def expand(coeffs, lo=0, hi=None):
+        high, low = split(coeffs)
+        return dot(bb[lo:hi, :], jnp.concatenate([high, low, high, jnp.zeros((8, 128), BF16)], 0))
+
+    hear(0)
+    tell(1)
+
+    pack(TOP, slots, jnp.concatenate([modes8[:, TOP:], jnp.zeros((32, slots - TOP), F32)], 0))
+    m_ref[TOP:, :] = expand(jnp.concatenate([start8, jnp.zeros((32, 128), F32)], 0), TOP)
+    loads[3].wait()
+    loads[4].wait()
+    r_ref[...] = rhs[...] - dot(ops[:, TOP:], m_ref[TOP:, :].astype(BF16))
 
     loads[2].wait()
     spread = (
@@ -133,32 +191,10 @@
     )
     hs[...] = (dot(high, spread) + dot(low, spread)).reshape(ncl, 8, wide)
     hb[i] = hs[i]
-    over_cluster(lambda peer: send(hs.at[peer], hb.at[i], h_sems, (peer, j)))
-
-    pad[...] = jnp.zeros_like(pad)
-    g_buf[:, :, 6:8, :] = jnp.zeros((3, nme, 2, 128), F32)
-    e_buf[:, :, 6:8, :] = jnp.zeros((2, nme, 2, 128), F32)
-    c_buf[:, :, 6:8, :] = jnp.zeros((3, 5, 2, 128), F32)
-
-    def pack(lo, hi, across):
-        high, low = split(across)
-        high, low = high.astype(F32), low.astype(F32)
-        none = jnp.zeros((8, hi - lo), F32)
-        bt[0:48, lo:hi] = jnp.concatenate([high, none], 0).astype(BF16)
-        bt[48:96, lo:hi] = jnp.concatenate([low, none], 0).astype(BF16)
-        bb[lo:hi, :] = jnp.concatenate([high, high, low, none], 0).T.astype(BF16)
-
-    def expand(coeffs, lo=0, hi=None):
-        high, low = split(coeffs)
-        return dot(bb[lo:hi, :], jnp.concatenate([high, low, high, jnp.zeros((8, 128), BF16)], 0))
-
-    pack(TOP, slots, jnp.concatenate([modes8[:, TOP:], jnp.zeros((32, slots - TOP), F32)], 0))
-    m_ref[TOP:, :] = expand(jnp.concatenate([start8, jnp.zeros((32, 128), F32)], 0), TOP)
-    loads[3].wait()
-    loads[4].wait()
-    r_ref[...] = rhs[...] - dot(ops[:, TOP:], m_ref[TOP:, :].astype(BF16))
 
     wait(s1_buf, s1_sems.at[1])
+    hear(1)
+    tell(2)
     across = [modes8[:, 0:TOP]]
     for f in range(4):
         block = jnp.concatenate([s1_buf[f, 0:8, :], jnp.zeros((8, TOP - 128), F32)], 1)
@@ -259,6 +295,8 @@
     r_ref[...] = r_ref[...] - dot(ops[:, 0:TOP], m_ref[0:TOP, :].astype(BF16))
     own = send_terms(times(bt, r_ref[...]), 0)
 
+    hear(2)
+    over_cluster(lambda peer: send(hs.at[peer], hb.at[i], h_sems, (peer, j)))
     gather(g_buf, g_sems, 0, own + received_terms(0))
     send_faces(r_ref, 0)
 
@@ -488,6 +526,7 @@
                 pltpu.VMEM((nme, 6, cases), F32),
                 pltpu.VMEM((ncl, 6, cases), F32),
                 pltpu.VMEM((6, cases), F32),
+                pltpu.SemaphoreType.REGULAR((3,)),
                 pltpu.SemaphoreType.DMA((8,)),
                 pltpu.SemaphoreType.DMA((2,)),
                 pltpu.SemaphoreType.DMA((2,)),

time: 70.3 us -> 68.7 us (0.977)
  Pallas kernels: 69.5 us -> 67.9 us
    pallas_call x1, Pallas kernels: 67.4 us -> 65.9 us  [per_device(): pl.pallas_call(functools.partial(kernel, ncl, nme, nx), out_shape=(out, o...]
where the time goes in v4:
time: 68.7 us; the launch traced here: 68.6 us
  Pallas kernels  67.9 us (99%)
    pallas_call x1, Pallas kernels, per_device(): pl.pallas_call(functools.partial(kernel, ncl, nme, nx), out_shape=(out, o...  65.9 us
    pallas_call x1, Pallas kernels, per_device(): pl.pallas_call(finish, out_shape=(out, out), in_specs=[pl.BlockSpec(memor...  2.09 us

profile of v4, /device:TPU:1, one launch (start us, length us, event | category | flops | bytes accessed | tf_op | source)
XLA Modules:
  0.0 68.6 jit_solution(14730931466792880426)
XLA Ops:
  0.6 65.9 %cg.1 = (f32[1024,128]{1,0:T(8,128)}, f32[1024,128]{1,0:T(8,128)}) custom-call(bf16[1024,1024]{1,0:T(8,128)(2,1)} %bitcast.8, f32[1024,128]{1,0:T(8,128)} %bitcast.9, f32[6,1,1024]{2,1,0:T(1,128)} %bitcast.11, f32[6,1,3072]{2,1,0:T(1,128)} %bitcast.10, f32[6,1,128]{2,1,0:T(1,128)} %bitcast.12, s32[4]{0:T(128)} %bitcast.13), custom_call_target="tpu_custom_call" | custom-call | tf_op jit(solution)/shard_map/cg/pallas_call | solution.py:485
  66.5 2.1 %finish.1 = (f32[1024,128]{1,0:T(8,128)}, f32[1024,128]{1,0:T(8,128)}) custom-call(f32[1024,128]{1,0:T(8,128)} %get-tuple-element.6.m_in, f32[1024,128]{1,0:T(8,128)} %get-tuple-element.7.p_in), custom_call_target="tpu_custom_call" | custom-call | tf_op jit(solution)/shard_map/finish/pallas_call | solution.py:553

commit v5 on v4

--- a/solution.py
+++ b/solution.py
@@ -319,9 +319,9 @@
     high, low = split(hb[...].reshape(8 * ncl, wide))
     h2[:, 0:wide] = high
     h2[:, wide : 2 * wide] = low
+    scatter(0)
     assemble(r_ref, 0)
     gr_own = send_terms(times(ft, r_ref[...]), 1)
-    scatter(0)
     for n, step in enumerate((2, 1)):
         send(hb.at[:, pl.ds(0, 6)], h_near.at[n, :, pl.ds(0, 6)], near_sems.at[n], at_step(step))
     gather(e_buf, e_sems, 0, gr_own + received_terms(1))
@@ -385,8 +385,8 @@
     assemble(im_ref, 1)
     gi_own = send_terms(times(ft, im_ref[...]), 2)
     sum_rows = [weighted(p0_ref[...]), inner_rows(p0_ref[...] * u0_ref[...])]
+    share(1)
     gather(e_buf, e_sems, 1, gi_own + received_terms(2))
-    share(1)
 
     q_ref[lower, :] = im_ref[lower, :] - expand(alone(1), TOP)
     v_ref[...] = apply(0.0, q_ref, lower)

time: 68.7 us -> 68.4 us (level)
  no operation moved by 1% of the time
where the time goes in v5:
time: 68.4 us; the launch traced here: 68.2 us
  Pallas kernels  67.5 us (99%)
    pallas_call x1, Pallas kernels, per_device(): pl.pallas_call(functools.partial(kernel, ncl, nme, nx), out_shape=(out, o...  65.5 us
    pallas_call x1, Pallas kernels, per_device(): pl.pallas_call(finish, out_shape=(out, out), in_specs=[pl.BlockSpec(memor...  2.09 us

profile of v5, /device:TPU:1, one launch (start us, length us, event | category | flops | bytes accessed | tf_op | source)
XLA Modules:
  0.0 68.2 jit_solution(4474491591113819314)
XLA Ops:
  0.6 65.5 %cg.1 = (f32[1024,128]{1,0:T(8,128)}, f32[1024,128]{1,0:T(8,128)}) custom-call(bf16[1024,1024]{1,0:T(8,128)(2,1)} %bitcast.8, f32[1024,128]{1,0:T(8,128)} %bitcast.9, f32[6,1,1024]{2,1,0:T(1,128)} %bitcast.11, f32[6,1,3072]{2,1,0:T(1,128)} %bitcast.10, f32[6,1,128]{2,1,0:T(1,128)} %bitcast.12, s32[4]{0:T(128)} %bitcast.13), custom_call_target="tpu_custom_call" | custom-call | tf_op jit(solution)/shard_map/cg/pallas_call | solution.py:485
  66.1 2.1 %finish.1 = (f32[1024,128]{1,0:T(8,128)}, f32[1024,128]{1,0:T(8,128)}) custom-call(f32[1024,128]{1,0:T(8,128)} %get-tuple-element.6.m_in, f32[1024,128]{1,0:T(8,128)} %get-tuple-element.7.p_in), custom_call_target="tpu_custom_call" | custom-call | tf_op jit(solution)/shard_map/finish/pallas_call | solution.py:553
